TPU v7x, 256 devices: a whole 4x4x8 slice. The times are simulated.
256 devices in a mesh: section: 8 (over z_hi, x), dp: 32 (over z_lo, y, core).
Axes of the slice: x: 4, y: 4, z: 8 (z_hi: 2, z_lo: 4; z = z_hi * 4 + z_lo), core: 2. Of those that a mesh axis runs over, the one named last changes fastest.
Arguments:
- inputs: bfloat16 [32, 128, 8192], P(None, 'dp'), may hold values from -16 to 16
- layer_gain: float32 [8, 8192], P('section'), may hold values from 0.5 to 1.5
- layer_down: bfloat16 [8, 8192, 128], P('section', 'dp'), may hold values from -0.0625 to 0.0625
- layer_up: bfloat16 [8, 128, 8192], P('section', None, 'dp'), may hold values from -0.5 to 0.5
- exit_norm_gain: float32 [8192], replicated, may hold values from 0.5 to 1.5
- head_weight: bfloat16 [8192, 16384], P('section', 'dp'), may hold values from -0.1875 to 0.1875
- targets: int32 [32, 128], replicated, may hold values from 0 to 16383
- exit_section: int32 [32], replicated, may hold values from 0 to 7, as said below
Outputs:
- exit_loss: float32 [8, 4, 128], P('section', None, 'dp')
Inputs may be any that keep to these rules, and one draw needn't show every extreme that they name: `exit_section`: each of the 8 sections is the exit of exactly 4 micro-batches.
All inputs are finite; a program needn't handle non-finite values.
Results may differ from a plain program's by a relative error of at most 0.0044.
Values may be sent and summed in bfloat16 or wider, within the bound.
No kernel may reach another device: no remote copies, remote signals or barrier semaphores. Data moves between devices by JAX's collectives and lax.ppermute only.
A program may use at most 128 MiB of HBM per device.

v0:
```python
import math

import functools

import jax
import jax.numpy as jnp
from jax import lax
from jax.experimental import pallas as pl
from jax.experimental.pallas import tpu as pltpu
from jax.sharding import Mesh, PartitionSpec as P

EPSILON = 1e-05
LOGIT_CEILING = 30.0
RECIPROCAL_HEAT = 1.0 / 0.7
INTERPRET = False

SECTION = ("zhi", "x")
DP = ("zlo", "y", "core")
PLANE = ("zlo", "y")
LINE = (0, 1, 2, 3)
RING = (0, 1, 3, 2)
F32, BF16 = jnp.float32, jnp.bfloat16


def hop(block, axis, bit):
    size = lax.axis_size(axis)
    return lax.ppermute(block, axis, [(i, i ^ bit) for i in range(size)])


def ring(low, high, axis):
    three_low = hop(low, axis, 3)
    one_high = hop(high, axis, 1)
    one_low = hop(low, axis, 1)
    three_high = hop(high, axis, 3)
    far_low = hop(three_low, axis, 1)
    far_high = hop(one_high, axis, 3)
    return [low, one_low, three_low, far_low], [high, one_high, three_high, far_high]


def tied(value, *others):
    return lax.optimization_barrier((value, *others))[0]


def spread(block, axis):
    size = lax.axis_size(axis)
    copies = jnp.broadcast_to(block[None], (size, *block.shape))
    return lax.all_to_all(copies, axis, 0, 0, tiled=True)


def direct(block, axis, order):
    return [block] + [hop(block, axis, bit) for bit in order[1:]]


def kernel_call(body, out, scalars, arrays, after=(), scratch=()):
    whole = pl.BlockSpec(memory_space=pltpu.VMEM)
    small = pl.BlockSpec(memory_space=pltpu.SMEM)
    unread = pl.BlockSpec(memory_space=pl.ANY)
    count = len(scalars) + len(arrays)

    def inner(*refs):
        body(*refs[:count], *refs[count + len(after) :])

    shapes = [jax.ShapeDtypeStruct(shape, dtype) for shape, dtype, _ in out]
    sizes = [math.prod(one.shape) * one.dtype.itemsize for one in [*shapes, *arrays]]
    limit = 6 + 5 * sum(sizes) // 2**22
    return pl.pallas_call(
        inner,
        out_shape=shapes,
        in_specs=[small] * len(scalars) + [whole] * len(arrays) + [unread] * len(after),
        out_specs=[whole if space == "v" else small for _, _, space in out],
        scratch_shapes=list(scratch),
        compiler_params=pltpu.CompilerParams(vmem_limit_bytes=limit * 2**20),
        interpret=INTERPRET,
    )(*scalars, *arrays, *after)


def gray(value):
    return value ^ (value >> 1)


def stack_kernel(*refs):
    out_ref = refs[-1]
    start = 0
    for ref in refs[:-1]:
        out_ref[start : start + ref.shape[0]] = ref[...]
        start += ref.shape[0]


def stack(pieces):
    total = sum(piece.shape[0] for piece in pieces)
    shape = (total, *pieces[0].shape[1:])
    return kernel_call(stack_kernel, [(shape, pieces[0].dtype, "v")], [], pieces)[0]


def block_at(where_ref, index):
    return (where_ref[2] ^ (index % 4)) * 4 + (where_ref[3] ^ gray(index // 4))


def rows_kernel(
    where_ref,
    exits_ref,
    inputs_ref,
    targets_ref,
    own_ref,
    other_ref,
    square_ref,
    rows_ref,
    wanted_ref,
    chosen_ref,
    count_ref,
):
    micro, tokens, width = inputs_ref.shape
    sections = 8
    exits = micro // sections
    each = exits * tokens
    zlo, y, core, section = where_ref[2], where_ref[3], where_ref[4], where_ref[5]
    for index in range(sections):
        count_ref[index] = 0
    for index in range(micro):
        place = exits_ref[index]
        spot = count_ref[place]
        count_ref[place] = spot + 1
        chosen_ref[place * exits + spot] = index
    for place in range(sections):
        parts = [inputs_ref[chosen_ref[place * exits + spot]].astype(F32) for spot in range(exits)]
        rows_ref[place * each : (place + 1) * each, :] = jnp.concatenate(parts, 0).astype(BF16)
    own = rows_ref[pl.ds(pl.multiple_of(section * each, each), each), :].astype(F32)
    square_ref[...] = jnp.sum(own * own, -1, keepdims=True)
    block = width // 32
    for index in range(16):
        start = block_at(where_ref, index) * 2 * block
        here = slice(index * block, (index + 1) * block)
        mine = pl.multiple_of(start + core * block, block)
        theirs = pl.multiple_of(start + (1 - core) * block, block)
        own_ref[:, here] = rows_ref[:, pl.ds(mine, block)]
        other_ref[:, here] = rows_ref[:, pl.ds(theirs, block)]
    lanes = targets_ref.shape[1]
    ids = [
        jnp.broadcast_to(targets_ref[pl.ds(chosen_ref[section * exits + spot], 1), :], (tokens, lanes))
        for spot in range(exits)
    ]
    ids = jnp.concatenate(ids * 16, 0)
    row = lax.broadcasted_iota(jnp.int32, ids.shape, 0)
    lane = lax.broadcasted_iota(jnp.int32, ids.shape, 1)
    ring_step = row // (4 * each)
    from_y = y ^ gray(ring_step)
    from_z = zlo ^ (row // each % 4)
    token = ((from_z * 4 + from_y) * 2 + core) * tokens + row % tokens
    wanted_ref[...] = jnp.sum(jnp.where(lane == token, ids, 0), -1, keepdims=True)


def state_kernel(where_ref, rows_ref, out_ref):
    each = out_ref.shape[0] // 2
    quarter = out_ref.shape[1] // 4
    zhi, x = where_ref[0], where_ref[1]
    for spot, half in ((0, 1 - zhi), (1, zhi)):
        begin = pl.multiple_of((half * 4 + x) * each, each)
        for index in range(4):
            start = pl.multiple_of((zhi * 4 + (x ^ gray(index))) * quarter, quarter)
            out_ref[spot * each : (spot + 1) * each, index * quarter : (index + 1) * quarter] = (
                rows_ref[pl.ds(begin, each), pl.ds(start, quarter)]
            )


def pair_kernel(first_ref, second_ref, out_ref):
    each = first_ref.shape[0] // 2
    out_ref[:each] = first_ref[:each]
    out_ref[each : 2 * each] = second_ref[:each]
    out_ref[2 * each : 3 * each] = first_ref[each:]
    out_ref[3 * each :] = second_ref[each:]


def part_kernel(first_ref, second_ref, low_ref, high_ref):
    each = first_ref.shape[0] // 2
    low_ref[:each] = first_ref[:each]
    low_ref[each:] = second_ref[:each]
    high_ref[:each] = first_ref[each:]
    high_ref[each:] = second_ref[each:]


def up_kernel(where_ref, came_ref, out_ref):
    block = came_ref.shape[2]
    for index in range(came_ref.shape[0]):
        piece = came_ref[block_at(where_ref, index)]
        for copy in range(out_ref.shape[0]):
            out_ref[copy, :, index * block : (index + 1) * block] = piece


def leaving_kernel(where_ref, lined_ref, out_ref):
    for z in range(2):
        at = ((1 - where_ref[0]) * 2 + z) ^ where_ref[2]
        out_ref[z] = lined_ref[at, :, out_ref.shape[2] :]


def products_kernel(where_ref, own_ref, other_ref, up_ref, *refs):
    pieces, (keep_ref, send_ref, stay_ref) = refs[:-3], refs[-3:]
    rows = own_ref.shape[0]
    rank = keep_ref.shape[1]
    zhi, zlo, core, section = where_ref[0], where_ref[2], where_ref[4], where_ref[5]
    total, start = 0.0, 0
    for piece in pieces:
        size = piece.shape[0] * piece.shape[1]
        here = slice(start, start + size)
        left = jnp.concatenate([own_ref[:, here], other_ref[:, here], up_ref[:, here]], 0)
        total += jnp.dot(left, piece[...].reshape(size, 2 * rank), preferred_element_type=F32)
        start += size
    each = rows // 8
    for ref, begin in ((keep_ref, 0), (send_ref, rows)):
        for index in range(8):
            part = total[begin + index * each : begin + (index + 1) * each]
            ref[index * 2 * each : (index * 2 + 1) * each] = part[:, :rank]
            ref[(index * 2 + 1) * each : (index * 2 + 2) * each] = part[:, rank:]
    up_rows = up_ref.shape[0] // 8
    layers = []
    for layer in range(8):
        part = total[2 * rows + layer * up_rows : 2 * rows + (layer + 1) * up_rows]
        layers.append(jnp.where(layer < section, part[:, :rank], part[:, rank:]))
    low = jnp.concatenate(layers[:4], 0)
    high = jnp.concatenate(layers[4:], 0)
    keep_ref[2 * rows :] = jnp.where(core == 0, low, high)
    send_ref[2 * rows :] = jnp.where(core == 0, high, low)
    for index, piece in enumerate(pieces):
        for z in range(2):
            stay_ref[z * 4 + index] = piece[(zhi * 2 + z) ^ zlo, :, rank:]


def combine_kernel(keep_ref, came_ref, out_ref):
    sections, each, _ = out_ref.shape
    half = each // 2
    shared = keep_ref[sections * half :] + came_ref[sections * half :]
    for index in range(sections):
        here = slice(index * half, (index + 1) * half)
        out_ref[index, :half] = keep_ref[here] + came_ref[here]
        out_ref[index, half:] = shared


def gram_kernel(incoming_ref, out_ref):
    sections, each, rank = incoming_ref.shape
    for index in range(sections):
        out_ref[:, index * rank : (index + 1) * rank] = incoming_ref[index, each // 2 :].astype(
            BF16
        )


def chain_kernel(where_ref, products_ref, gram_ref, square_ref, sent_ref, latent_ref):
    layers, each, rank = products_ref.shape
    rows = each // 4
    width = where_ref[6].astype(F32)
    square = square_ref[...]
    for layer in range(layers):
        here = slice(layer * rank, (layer + 1) * rank)
        before = slice(0, layer * rank)
        entering = products_ref[layer, :rows]
        cross = products_ref[layer, rows : 2 * rows]
        if layer > 0:
            earlier = latent_ref[:, before]
            entering += jnp.dot(earlier, gram_ref[before, here], preferred_element_type=F32)
            cross += lax.dot_general(
                earlier,
                gram_ref[here, before],
                (((1,), (1,)), ((), ())),
                preferred_element_type=F32,
            )
        value = entering * lax.rsqrt(square / width + EPSILON)
        latent = (value / (1.0 + jnp.exp(-value))).astype(BF16)
        latent = jnp.where(layer <= where_ref[5], latent, jnp.zeros_like(latent))
        latent_ref[:, here] = latent
        spot = layer // 4 * 4 + gray(where_ref[1] ^ (layer % 4))
        sent_ref[:, pl.ds(pl.multiple_of(spot * rank, rank), rank)] = latent
        own = jnp.dot(latent, gram_ref[here, here], preferred_element_type=F32)
        grown = latent.astype(F32) * (2.0 * cross + own)
        square = jnp.maximum(square + jnp.sum(grown, -1, keepdims=True), 0.0)
    scale = lax.rsqrt(square / width + EPSILON)
    scale = jnp.broadcast_to(scale, (rows, rank))
    lane = lax.broadcasted_iota(jnp.int32, (rows, rank), 1)
    high = scale.astype(BF16).astype(F32)
    middle = (scale - high).astype(BF16).astype(F32)
    low = scale - high - middle
    parts = jnp.where(lane == 0, high, jnp.where(lane == 1, middle, low))
    parts = jnp.where(lane < 3, parts, 0.0)
    sent_ref[:, layers * rank :] = parts.astype(BF16)


def head_kernel(*refs):
    pieces, (head_ref, other_ref, out_ref) = refs[:-3], refs[-3:]
    left = jnp.concatenate([piece[...] for piece in pieces], 0)
    half = head_ref.shape[1]
    out_ref[:, :half] = jnp.dot(left, head_ref[...], preferred_element_type=F32).astype(
        out_ref.dtype
    )
    out_ref[:, half:] = jnp.dot(left, other_ref[...], preferred_element_type=F32).astype(
        out_ref.dtype
    )


def correction_kernel(where_ref, own_ref, *refs):
    came_refs, (head_ref, other_ref, keep_ref, send_ref) = refs[:4], refs[4:]
    blocks, block, rank = own_ref.shape
    half = head_ref.shape[1]
    zhi, x, y, core = where_ref[0], where_ref[1], where_ref[3], where_ref[4]
    totals = [0.0, 0.0]
    for index in range(blocks):
        at = index // 4 * 4 + (y ^ gray(index % 4))
        start = gray(x ^ (at // 2)) * 4 + at % 2 * 2 + core
        here = pl.ds(pl.multiple_of(start * block, block), block)
        maps = jnp.concatenate([own_ref[index], came_refs[index % 4][index // 4]], 1)
        for spot, ref in enumerate((head_ref, other_ref)):
            totals[spot] += lax.dot_general(
                maps, ref[here, :], (((0,), (0,)), ((), ())), preferred_element_type=F32
            )
    for spot, total in enumerate(totals):
        mine = jnp.where(core == zhi, total[:rank], total[rank:])
        theirs = jnp.where(core == zhi, total[rank:], total[:rank])
        keep_ref[:, spot * half : (spot + 1) * half] = mine
        send_ref[:, (1 - spot) * half : (2 - spot) * half] = theirs.astype(BF16)


def losses_kernel(
    where_ref, latents_ref, own_ref, other_ref, base_ref, came_ref, wanted_ref, out_ref
):
    zlo, y, core = where_ref[2], where_ref[3], where_ref[4]
    places = [(zlo ^ (index % 4)) * 4 + (y ^ gray(index // 4)) for index in range(16)]
    latents = jnp.concatenate([latents_ref[place] for place in places], 0)
    depth, columns = own_ref.shape
    half = columns // 2
    scale = jnp.sum(latents[:, 2 * depth :].astype(F32), -1, keepdims=True)
    low, high = latents[:, :depth], latents[:, depth : 2 * depth]
    mine = jnp.where(core == 0, low, high)
    theirs = jnp.where(core == 0, high, low)
    exp_total, picked = 0.0, 0.0
    for spot in range(2):
        here = slice(spot * half, (spot + 1) * half)
        there = slice((1 - spot) * half, (2 - spot) * half)
        logits = base_ref[:, here] + came_ref[:, here].astype(F32)
        logits += jnp.dot(mine, own_ref[:, here], preferred_element_type=F32)
        logits += jnp.dot(theirs, other_ref[:, there], preferred_element_type=F32)
        capped = LOGIT_CEILING * jnp.tanh(logits * scale * RECIPROCAL_HEAT / LOGIT_CEILING)
        exp_total += jnp.sum(jnp.exp(capped), -1, keepdims=True)
        begin = ((zlo * 4 + y) * 2 + (core ^ spot)) * half
        column = begin + lax.broadcasted_iota(jnp.int32, capped.shape, 1)
        picked += jnp.sum(jnp.where(column == wanted_ref[...], capped, 0.0), -1, keepdims=True)
    plane, each, lanes = out_ref.shape
    lane = lax.broadcasted_iota(jnp.int32, (plane * each, lanes), 1)
    sums = jnp.where(lane == 0, exp_total, jnp.where(lane == 1, picked, 0.0))
    for index, place in enumerate(places):
        out_ref[place] = sums[index * each : (index + 1) * each]


def finish_kernel(sums_ref, out_ref):
    total = sums_ref[0]
    for index in range(1, sums_ref.shape[0]):
        total += sums_ref[index]
    out_ref[...] = jnp.log(total[:, :1]) - total[:, 1:2]


def per_device(
    inputs, layer_gain, layer_down, layer_up, exit_norm_gain, head_weight, targets, exit_section
):
    section = lax.axis_index(SECTION)
    place = lax.axis_index(DP)
    zhi, x, zlo, y, core = (lax.axis_index(name) for name in SECTION + DP)
    micro, tokens, width = inputs.shape
    sections = lax.axis_size(SECTION)
    plane = lax.axis_size(PLANE)
    rank = layer_up.shape[1]
    own_rank = rank // plane
    exits = micro // sections
    rows = exits * tokens
    head_rows, head_columns = head_weight.shape
    where = jnp.stack([zhi, x, zlo, y, core, section, jnp.int32(width)]).astype(jnp.int32)

    head_gain = lax.dynamic_slice_in_dim(exit_norm_gain, section * head_rows, head_rows, 0)
    scaled_head = (head_weight.astype(F32) * head_gain[:, None]).astype(BF16)

    up = layer_up[0]
    features = up.shape[1]
    came = lax.all_to_all(up, PLANE, 0, 0, tiled=True).reshape(plane, own_rank, features)

    gain = lax.dynamic_slice_in_dim(layer_gain[0], place * features, features, 0)
    scaled_down = (layer_down[0].astype(F32) * gain[:, None]).astype(BF16)
    pair = jnp.concatenate([scaled_down, up.T], 1)
    lined = direct(pair, "zlo", LINE)

    half_rows = ((sections * rows, width // 2), BF16, "v")
    own_rows, other_rows, own_square, all_rows, wanted, _ = kernel_call(
        rows_kernel,
        [
            half_rows,
            half_rows,
            ((rows, 1), F32, "v"),
            ((sections * rows, width), BF16, "v"),
            ((plane * rows, 1), jnp.int32, "v"),
            ((micro,), jnp.int32, "s"),
        ],
        [where, tied(exit_section, came)],
        [inputs, targets],
        scratch=[pltpu.SMEM((sections,), jnp.int32)],
    )
    lined = stack([tied(piece, came)[None] for piece in lined])
    maps = direct(lined, "y", RING)

    (leaving,) = kernel_call(
        leaving_kernel, [((2, features, rank), BF16, "v")], [where], [lined]
    )
    up_came = hop(leaving, "zhi", 1)
    partner_rows = hop(tied(other_rows, up_came), "core", 1)

    (state,) = kernel_call(
        state_kernel, [((2 * rows, width // 2), BF16, "v")], [where], [all_rows]
    )
    state = tied(state, up_came)
    (state,) = kernel_call(
        pair_kernel, [((4 * rows, width // 2), BF16, "v")], [], [state, hop(state, "zlo", 1)]
    )
    state = [state, hop(state, "zlo", 2)]

    (copies,) = kernel_call(
        up_kernel, [((sections, own_rank, width // 2), BF16, "v")], [where], [came]
    )
    copies = tied(copies, up_came)
    up_rows = lax.all_to_all(copies, SECTION, 0, 0, tiled=True)
    up_rows = up_rows.reshape(sections * own_rank, width // 2)

    up_came = direct(tied(up_came, *maps), "y", RING)

    sums = ((2 * sections * rows + 4 * own_rank, rank), F32, "v")
    keep, send, up_stay = kernel_call(
        products_kernel,
        [sums, sums, ((plane // 2, features, rank), BF16, "v")],
        [where],
        [own_rows, partner_rows, up_rows, *maps],
    )
    (outgoing,) = kernel_call(
        combine_kernel, [((sections, 4 * rows, rank), F32, "v")], [], [keep, hop(send, "core", 1)]
    )
    head_pieces = direct(tied(scaled_head, up_rows), "x", RING)
    line_rows = ((4 * rows, width // 2), BF16, "v")
    state = kernel_call(part_kernel, [line_rows, line_rows], [], [tied(part, send) for part in state])
    passing, staying = ring(*state, "y")

    outgoing = tied(outgoing, *up_came, *state)
    incoming = lax.all_to_all(outgoing, SECTION, 0, 0, tiled=True)
    (gram,) = kernel_call(
        gram_kernel, [((4 * own_rank, sections * rank), BF16, "v")], [], [incoming]
    )
    gram = spread(tied(gram, *passing[1:3], *staying[1:3]), "zlo")
    gram = spread(tied(gram, passing[3], staying[3]), "y").reshape(-1, sections * rank)
    head = stack([tied(piece, incoming) for piece in head_pieces])
    other_head = hop(head, "core", 1)
    wide = 2 * head_columns
    mine, theirs = kernel_call(
        correction_kernel,
        [((rank, wide), F32, "v"), ((rank, wide), BF16, "v")],
        [where],
        [up_stay, *up_came, head, other_head],
    )
    mine = mine + hop(theirs, "core", 1).astype(F32)
    mine = (mine + hop(mine.astype(BF16), "zhi", 1).astype(F32)).astype(BF16)
    correction = direct(mine, "x", RING)

    def through(pieces, dtype):
        shape = (plane * rows, wide)
        return kernel_call(
            head_kernel, [(shape, dtype, "v")], [], [*pieces, head, other_head]
        )[0]

    passing = through(passing, BF16)
    passed = hop(passing, "zhi", 1)
    base = through(staying, F32)

    gram = tied(gram, mine, passing, staying[3])
    steps = jnp.arange(4, dtype=jnp.int32)
    at = ((steps[None, :] * 4 + steps[:, None]) * own_rank)[..., None, None]
    at = at + (steps * rank)[:, None] + jnp.arange(own_rank, dtype=jnp.int32)
    at = at.reshape(-1)
    line = jnp.arange(sections * rank, dtype=jnp.int32)[:, None]
    own_sorting = (line == (at + core * 4 * rank)[None, :]).astype(BF16)
    other_sorting = (line == (at + (1 - core) * 4 * rank)[None, :]).astype(BF16)
    gram = jnp.dot(own_sorting, gram, preferred_element_type=F32) + jnp.dot(
        other_sorting, hop(gram, "core", 1), preferred_element_type=F32
    )
    (latents,) = kernel_call(
        chain_kernel,
        [((rows, (sections + 1) * rank), BF16, "v")],
        [where],
        [incoming, gram.astype(BF16), own_square],
        scratch=[pltpu.VMEM((rows, sections * rank), BF16)],
    )

    latents = spread(tied(latents, passed, *correction), PLANE)
    correction = stack(correction)
    other_correction = hop(correction, "core", 1)
    (sums,) = kernel_call(
        losses_kernel,
        [((plane, rows, rank), F32, "v")],
        [where],
        [latents, correction, other_correction, base, passed, wanted],
    )
    sums = lax.all_to_all(sums, PLANE, 0, 0, tiled=True)
    (losses,) = kernel_call(finish_kernel, [((rows, 1), F32, "v")], [], [sums])
    return losses.reshape(1, exits, tokens)


def solution(mesh):
    split = Mesh(mesh.devices.reshape(2, 4, 4, 4, 2), SECTION + DP)
    placed = (
        P(None, DP, None),
        P(SECTION, None),
        P(SECTION, DP, None),
        P(SECTION, None, DP),
        P(),
        P(SECTION, DP),
        P(),
        P(),
    )
    return jax.shard_map(
        per_device, mesh=split, in_specs=placed, out_specs=P(SECTION, None, DP), check_vma=False
    )
```

profile of v0, /device:TPU:2, one launch (start us, length us, event | category | flops | bytes accessed | tf_op | source)
XLA Modules:
  0.0 251.3 jit_solution(12600151381326958874)
XLA Ops:
  2.0 4.7 %collective-permute-start.2 = (bf16[256,256]{1,0:T(8,128)(2,1)S(1)}, bf16[256,256]{1,0:T(8,128)(2,1)S(1)}, u32[]{:S(2)}, u32[]{:S(2)}) collective-permute-start(bf16[256,256]{1,0:T(8,128)(2,1)S(1)} %pad_maximum_fusion), channel_id=1, source_target_pairs={{0,24},{8,16},{16,8},{24,0},{1,25},{9,17},{17,9},{25,1},{2,26},{10... | collective-permute-start | bytes 393224 | tf_op jit(solution)/shard_map/ppermute | solution.py:27
  7.4 7.7 %all-to-all-start = ((bf16[16,8,256]{2,1,0:T(8,128)(2,1)}), bf16[16,8,256]{2,1,0:T(8,128)(2,1)S(1)}, u32[]{:S(2)}, u32[]{:S(2)}) async-start(bf16[16,8,256]{2,1,0:T(8,128)(2,1)} %bitcast.27), calls=%async_computation | async-start | bytes 131072 | tf_op jit(solution)/shard_map/all_to_all | solution.py:377
  15.2 8.3 %all-to-all-done.refs_1_ = bf16[16,8,256]{2,1,0:T(8,128)(2,1)S(1)} async-done(((bf16[16,8,256]{2,1,0:T(8,128)(2,1)}), bf16[16,8,256]{2,1,0:T(8,128)(2,1)S(1)}, u32[]{:S(2)}, u32[]{:S(2)}) %all-to-all-start) | async-done | bytes 65568 | tf_op jit(solution)/shard_map/all_to_all | solution.py:377
  24.2 4.6 %collective-permute-start.3 = (bf16[2,256,128]{2,1,0:T(8,128)(2,1)S(1)}, bf16[2,256,128]{2,1,0:T(8,128)(2,1)S(1)}, u32[]{:S(2)}, u32[]{:S(2)}) collective-permute-start(bf16[2,256,128]{2,1,0:T(8,128)(2,1)S(1)} %shard_map.84), channel_id=1, source_target_pairs={{0,128},{128,0},{1,129},{129,1},{2,130},{130,2},{3,131},{131,3},{4... | collective-permute-start | bytes 393224 | tf_op jit(solution)/shard_map/ppermute | solution.py:27
  28.7 1.4 shard_map.85
  30.1 3.9 %collective-permute-done.3.refs_2_ = bf16[2,256,128]{2,1,0:T(8,128)(2,1)S(1)} collective-permute-done((bf16[2,256,128]{2,1,0:T(8,128)(2,1)S(1)}, bf16[2,256,128]{2,1,0:T(8,128)(2,1)S(1)}, u32[]{:S(2)}, u32[]{:S(2)}) %collective-permute-start.3) | collective-permute-done | bytes 131104 | tf_op jit(solution)/shard_map/ppermute | solution.py:27
  34.0 8.3 %all-to-all-start.1 = ((bf16[8,8,4096]{2,1,0:T(8,128)(2,1)}), bf16[8,8,4096]{2,1,0:T(8,128)(2,1)S(1)}, u32[]{:S(2)}, u32[]{:S(2)}) async-start(bf16[8,8,4096]{2,1,0:T(8,128)(2,1)} %shard_map.85), calls=%async_computation.1 | async-start | bytes 1048576 | tf_op jit(solution)/shard_map/all_to_all | solution.py:421
  42.3 1.6 copy-done.1
  43.9 3.0 %shard_map.82 = (bf16[128,4096]{1,0:T(8,128)(2,1)S(1)}, bf16[128,4096]{1,0:T(8,128)(2,1)}, f32[16,1]{1,0:T(8,128)S(1)}, bf16[128,8192]{1,0:T(8,128)(2,1)S(1)}, s32[256,1]{1,0:T(8,128)S(1)}, /*index=5*/s32[32]{0:T(128)}) custom-call(s32[7]{0:T(128)S(1)} %stack.27.refs_0_, s32[32]{0:T(128)S(1)} %copy-done.29, bf16[32,4,8192]{2,1,0:T(4,128)(2,1)S(1)} %copy-done.1, ...), custom_call_target="tpu_custom_call" | custom-call | tf_op jit(solution)/shard_map/pallas_call | solution.py:66
  48.5 1.5 collective-permute-start.7
  52.7 5.4 %collective-permute-done.12.refs_1_ = bf16[32,4096]{1,0:T(8,128)(2,1)S(1)} collective-permute-done((bf16[32,4096]{1,0:T(8,128)(2,1)S(1)}, bf16[32,4096]{1,0:T(8,128)(2,1)S(1)}, u32[]{:S(2)}, u32[]{:S(2)}) %collective-permute-start.12) | collective-permute-done | bytes 262176 | tf_op jit(solution)/shard_map/ppermute | solution.py:27
  58.2 2.2 collective-permute-start.13
  60.4 1.5 multiply_convert_fusion.refs_0_
  61.9 2.9 %collective-permute-done.7.refs_7_ = bf16[4,256,256]{2,1,0:T(8,128)(2,1)S(1)} collective-permute-done((bf16[4,256,256]{2,1,0:T(8,128)(2,1)S(1)}, bf16[4,256,256]{2,1,0:T(8,128)(2,1)S(1)}, u32[]{:S(2)}, u32[]{:S(2)}) %collective-permute-start.7) | collective-permute-done | bytes 524320 | tf_op jit(solution)/shard_map/ppermute | solution.py:27
  64.8 2.1 collective-permute-start.22
  66.9 8.5 %collective-permute-done.6.refs_6_ = bf16[4,256,256]{2,1,0:T(8,128)(2,1)} collective-permute-done((bf16[4,256,256]{2,1,0:T(8,128)(2,1)S(1)}, bf16[4,256,256]{2,1,0:T(8,128)(2,1)}, u32[]{:S(2)}, u32[]{:S(2)}) %collective-permute-start.6) | collective-permute-done | bytes 524320 | tf_op jit(solution)/shard_map/ppermute | solution.py:27
  75.4 1.5 collective-permute-start.21
  76.9 1.8 collective-permute-start.20
  78.7 1.5 collective-permute-start.11
  81.4 2.4 shard_map.86
  83.9 1.3 collective-permute-done.11.refs_5_
  87.8 4.5 %collective-permute-done.10.refs_4_ = bf16[2,256,128]{2,1,0:T(8,128)(2,1)S(1)} collective-permute-done((bf16[2,256,128]{2,1,0:T(8,128)(2,1)S(1)}, bf16[2,256,128]{2,1,0:T(8,128)(2,1)S(1)}, u32[]{:S(2)}, u32[]{:S(2)}) %collective-permute-start.10) | collective-permute-done | bytes 131104 | tf_op jit(solution)/shard_map/ppermute | solution.py:27
  92.3 23.1 %all_to_all.39.refs_0_.refs_1_ = f32[8,64,128]{2,1,0:T(8,128)S(1)} all-to-all(f32[8,64,128]{2,1,0:T(8,128)S(1)} %shard_map.87), channel_id=1, replica_groups=mesh['zhi'=2,'x'=4,'zlo'=4,'y'=4,'core'=2] {'zhi','x'}, dimensions={0} | all-to-all | bytes 524288 | tf_op jit(solution)/shard_map/all_to_all | solution.py:442
  115.5 2.3 shard_map.92.refs_6_.refs_4_
  119.4 1.3 collective-permute-start.14
  120.6 2.4 collective-permute-start.17
  123.0 10.8 %collective-permute-done.15.refs_2_ = bf16[64,4096]{1,0:T(8,128)(2,1)} collective-permute-done((bf16[64,4096]{1,0:T(8,128)(2,1)S(1)}, bf16[64,4096]{1,0:T(8,128)(2,1)}, u32[]{:S(2)}, u32[]{:S(2)}) %collective-permute-start.15) | collective-permute-done | bytes 524320 | tf_op jit(solution)/shard_map/ppermute | solution.py:27
  133.8 2.0 collective-permute-start.19
  135.8 8.9 %collective-permute-done.14.refs_1_ = bf16[64,4096]{1,0:T(8,128)(2,1)S(1)} collective-permute-done((bf16[64,4096]{1,0:T(8,128)(2,1)S(1)}, bf16[64,4096]{1,0:T(8,128)(2,1)S(1)}, u32[]{:S(2)}, u32[]{:S(2)}) %collective-permute-start.14) | collective-permute-done | bytes 524320 | tf_op jit(solution)/shard_map/ppermute | solution.py:27
  146.2 4.0 %all-to-all-start.3 = ((bf16[4,32,1024]{2,1,0:T(8,128)(2,1)}), bf16[4,32,1024]{2,1,0:T(8,128)(2,1)}, u32[]{:S(2)}, u32[]{:S(2)}) async-start(bf16[4,32,1024]{2,1,0:T(8,128)(2,1)} %broadcast_in_dim.18), calls=%async_computation.3 | async-start | bytes 524288 | tf_op jit(solution)/shard_map/all_to_all | solution.py:47
  150.3 5.5 %shard_map.93 = (f32[128,1024]{1,0:T(8,128)S(1)}, bf16[128,1024]{1,0:T(8,128)(2,1)}) custom-call(s32[7]{0:T(128)S(1)} %stack.27.refs_0_, bf16[8,256,128]{2,1,0:T(8,128)(2,1)S(1)} %copy-done.13, bf16[2,256,128]{2,1,0:T(8,128)(2,1)S(1)} %collective-permute-done.3.refs_2_, bf16[2,256,128]{2,1,0:T(8,128)(2,1)S(1)} %copy-done.25, ...), custom_call_target="tpu_custom_call" | custom-call | tf_op jit(solution)/shard_map/pallas_call | solution.py:66
  155.8 2.7 %all-to-all-done.3 = bf16[4,32,1024]{2,1,0:T(8,128)(2,1)} async-done(((bf16[4,32,1024]{2,1,0:T(8,128)(2,1)}), bf16[4,32,1024]{2,1,0:T(8,128)(2,1)}, u32[]{:S(2)}, u32[]{:S(2)}) %all-to-all-start.3) | async-done | bytes 262176 | tf_op jit(solution)/shard_map/all_to_all | solution.py:47
  158.5 2.2 broadcast_in_dim.19
  160.7 4.2 %all-to-all-start.4 = ((bf16[4,4,32,1024]{3,2,1,0:T(8,128)(2,1)}), bf16[4,4,32,1024]{3,2,1,0:T(8,128)(2,1)}, u32[]{:S(2)}, u32[]{:S(2)}) async-start(bf16[4,4,32,1024]{3,2,1,0:T(8,128)(2,1)} %broadcast_in_dim.19), calls=%async_computation.4 | async-start | bytes 2097152 | tf_op jit(solution)/shard_map/all_to_all | solution.py:47
  165.1 5.5 %collective-permute-start.25 = (bf16[128,1024]{1,0:T(8,128)(2,1)S(1)}, bf16[128,1024]{1,0:T(8,128)(2,1)S(1)}, u32[]{:S(2)}, u32[]{:S(2)}) collective-permute-start(bf16[128,1024]{1,0:T(8,128)(2,1)S(1)} %fusion.3), channel_id=1, source_target_pairs={{0,128},{128,0},{1,129},{129,1},{2,130},{130,2},{3,131},{131,3},{4... | collective-permute-start | bytes 786440 | tf_op jit(solution)/shard_map/ppermute | solution.py:27
  171.6 6.1 %shard_map.94 = bf16[256,1024]{1,0:T(8,128)(2,1)S(1)} custom-call(bf16[64,4096]{1,0:T(8,128)(2,1)S(1)} %copy-done.17, bf16[64,4096]{1,0:T(8,128)(2,1)S(1)} %copy-done.19, bf16[64,4096]{1,0:T(8,128)(2,1)} %collective-permute-done.15.refs_2_, bf16[64,4096]{1,0:T(8,128)(2,1)} %collective-permute-done.18.refs_3_, bf16[4096,512]{1,0:T(8,128)(2,1)} %shard_map.92.refs_6_.refs_4_, ...), custom_call_target="tpu_custom_call" | custom-call | tf_op jit(solution)/shard_map/pallas_call | solution.py:66
  178.8 5.5 %collective-permute-start.27 = (bf16[256,1024]{1,0:T(8,128)(2,1)S(1)}, bf16[256,1024]{1,0:T(8,128)(2,1)S(1)}, u32[]{:S(2)}, u32[]{:S(2)}) collective-permute-start(bf16[256,1024]{1,0:T(8,128)(2,1)S(1)} %shard_map.94), channel_id=1, source_target_pairs={{0,128},{128,0},{1,129},{129,1},{2,130},{130,2},{3,131},{131,3},{4... | collective-permute-start | bytes 1572872 | tf_op jit(solution)/shard_map/ppermute | solution.py:27
  184.3 2.1 collective-permute-start.30
  186.3 2.5 collective-permute-start.29
  189.0 2.5 fusion
  191.5 2.5 %add_convert_fusion.refs_2_ = bf16[1024,1024]{1,0:T(8,128)(2,1)S(1)} fusion(f32[1024,1024]{1,0:T(8,128)S(1)} %fusion, bf16[512,1024]{1,0:T(8,128)(2,1)} %bitcast.16, s32[512]{0:T(512)S(1)} %add.140), kind=kOutput, calls=%fused_computation | convolution fusion | flops 1076363264 | bytes 7342080 | tf_op jit(solution)/shard_map/dot_general | solution.py:479
  194.0 2.9 %shard_map.95 = bf16[16,1152]{1,0:T(8,128)(2,1)S(1)} custom-call(s32[7]{0:T(128)S(1)} %stack.27.refs_0_, f32[8,64,128]{2,1,0:T(8,128)S(1)} %all_to_all.39.refs_0_.refs_1_, bf16[1024,1024]{1,0:T(8,128)(2,1)S(1)} %add_convert_fusion.refs_2_, f32[16,1]{1,0:T(8,128)S(1)} %get-tuple-element.68.refs_3_), custom_call_target="tpu_custom_call" | custom-call | tf_op jit(solution)/shard_map/pallas_call | solution.py:66
  197.3 2.5 %collective-permute-done.29.refs_2_ = bf16[128,1024]{1,0:T(8,128)(2,1)S(1)} collective-permute-done((bf16[128,1024]{1,0:T(8,128)(2,1)S(1)}, bf16[128,1024]{1,0:T(8,128)(2,1)S(1)}, u32[]{:S(2)}, u32[]{:S(2)}) %collective-permute-start.29) | collective-permute-done | bytes 262176 | tf_op jit(solution)/shard_map/ppermute | solution.py:27
  200.8 15.5 %all-to-all-start.5 = ((bf16[16,16,1152]{2,1,0:T(8,128)(2,1)}), bf16[16,16,1152]{2,1,0:T(8,128)(2,1)S(1)}, u32[]{:S(2)}, u32[]{:S(2)}) async-start(bf16[16,16,1152]{2,1,0:T(8,128)(2,1)} %broadcast_in_dim.20), calls=%async_computation.5 | async-start | bytes 1179648 | tf_op jit(solution)/shard_map/all_to_all | solution.py:47
  220.5 5.8 %shard_map.97.refs_4_ = f32[256,1024]{1,0:T(8,128)S(1)} custom-call(bf16[64,4096]{1,0:T(8,128)(2,1)S(1)} %get-tuple-element.55.refs_0_, bf16[64,4096]{1,0:T(8,128)(2,1)S(1)} %copy-done.7, bf16[64,4096]{1,0:T(8,128)(2,1)S(1)} %copy-done.9, bf16[64,4096]{1,0:T(8,128)(2,1)S(1)} %copy-done.11, bf16[4096,512]{1,0:T(8,128)(2,1)} %shard_map.92.refs_6_.refs_4_, ...), custom_call_target="tpu_custom_call" | custom-call | tf_op jit(solution)/shard_map/pallas_call | solution.py:66
  227.4 5.6 %all-to-all-done.5.refs_1_ = bf16[16,16,1152]{2,1,0:T(8,128)(2,1)S(1)} async-done(((bf16[16,16,1152]{2,1,0:T(8,128)(2,1)}), bf16[16,16,1152]{2,1,0:T(8,128)(2,1)S(1)}, u32[]{:S(2)}, u32[]{:S(2)}) %all-to-all-start.5) | async-done | bytes 589856 | tf_op jit(solution)/shard_map/all_to_all | solution.py:47
  235.3 1.7 shard_map.98
  237.0 13.4 %all_to_all.40.refs_0_ = f32[16,16,128]{2,1,0:T(8,128)S(1)} all-to-all(f32[16,16,128]{2,1,0:T(8,128)S(1)} %shard_map.98), channel_id=1, replica_groups=mesh['zhi'=2,'x'=4,'zlo'=4,'y'=4,'core'=2] {'zlo','y'}, dimensions={0} | all-to-all | bytes 262144 | tf_op jit(solution)/shard_map/all_to_all | solution.py:499
  (129 shorter events, 26.9 us)
Async XLA Ops:
  0.0 42.3 %copy-start.29 = (s32[32]{0:T(128)S(1)}, s32[32]{0:T(128)}, u32[]{:S(2)}) copy-start(s32[32]{0:T(128)} %refs_1_) | copy-start | bytes 388
  0.0 42.3 %copy-start.28 = (s32[32,128]{1,0:T(8,128)S(1)}, s32[32,128]{1,0:T(8,128)}, u32[]{:S(2)}) copy-start(s32[32,128]{1,0:T(8,128)} %refs_3_.1) | copy-start | bytes 49156
  2.0 21.5 %collective-permute-start.2 = (bf16[256,256]{1,0:T(8,128)(2,1)S(1)}, bf16[256,256]{1,0:T(8,128)(2,1)S(1)}, u32[]{:S(2)}, u32[]{:S(2)}) collective-permute-start(bf16[256,256]{1,0:T(8,128)(2,1)S(1)} %pad_maximum_fusion), channel_id=1, source_target_pairs={{0,24},{8,16},{16,8},{24,0},{1,25},{9,17},{17,9},{25,1},{2,26},{10... | collective-permute-start | bytes 393224 | tf_op jit(solution)/shard_map/ppermute | solution.py:27
  6.7 16.8 %collective-permute-start.1 = (bf16[256,256]{1,0:T(8,128)(2,1)S(1)}, bf16[256,256]{1,0:T(8,128)(2,1)S(1)}, u32[]{:S(2)}, u32[]{:S(2)}) collective-permute-start(bf16[256,256]{1,0:T(8,128)(2,1)S(1)} %pad_maximum_fusion), channel_id=1, source_target_pairs={{0,16},{8,24},{16,0},{24,8},{1,17},{9,25},{17,1},{25,9},{2,18},{10... | collective-permute-start | bytes 393224 | tf_op jit(solution)/shard_map/ppermute | solution.py:27
  6.7 16.8 %collective-permute-start = (bf16[256,256]{1,0:T(8,128)(2,1)S(1)}, bf16[256,256]{1,0:T(8,128)(2,1)S(1)}, u32[]{:S(2)}, u32[]{:S(2)}) collective-permute-start(bf16[256,256]{1,0:T(8,128)(2,1)S(1)} %pad_maximum_fusion), channel_id=1, source_target_pairs={{0,8},{8,0},{16,24},{24,16},{1,9},{9,1},{17,25},{25,17},{2,10},{10... | collective-permute-start | bytes 393224 | tf_op jit(solution)/shard_map/ppermute | solution.py:27
  7.4 16.1 %all-to-all-start = ((bf16[16,8,256]{2,1,0:T(8,128)(2,1)}), bf16[16,8,256]{2,1,0:T(8,128)(2,1)S(1)}, u32[]{:S(2)}, u32[]{:S(2)}) async-start(bf16[16,8,256]{2,1,0:T(8,128)(2,1)} %bitcast.27), calls=%async_computation | async-start | bytes 131072 | tf_op jit(solution)/shard_map/all_to_all | solution.py:377
  24.2 9.8 %collective-permute-start.3 = (bf16[2,256,128]{2,1,0:T(8,128)(2,1)S(1)}, bf16[2,256,128]{2,1,0:T(8,128)(2,1)S(1)}, u32[]{:S(2)}, u32[]{:S(2)}) collective-permute-start(bf16[2,256,128]{2,1,0:T(8,128)(2,1)S(1)} %shard_map.84), channel_id=1, source_target_pairs={{0,128},{128,0},{1,129},{129,1},{2,130},{130,2},{3,131},{131,3},{4... | collective-permute-start | bytes 393224 | tf_op jit(solution)/shard_map/ppermute | solution.py:27
  34.0 27.9 %all-to-all-start.1 = ((bf16[8,8,4096]{2,1,0:T(8,128)(2,1)}), bf16[8,8,4096]{2,1,0:T(8,128)(2,1)S(1)}, u32[]{:S(2)}, u32[]{:S(2)}) async-start(bf16[8,8,4096]{2,1,0:T(8,128)(2,1)} %shard_map.85), calls=%async_computation.1 | async-start | bytes 1048576 | tf_op jit(solution)/shard_map/all_to_all | solution.py:421
  46.8 31.8 %collective-permute-start.4 = (bf16[128,4096]{1,0:T(8,128)(2,1)}, bf16[128,4096]{1,0:T(8,128)(2,1)}, u32[]{:S(2)}, u32[]{:S(2)}) collective-permute-start(bf16[128,4096]{1,0:T(8,128)(2,1)} %get-tuple-element.45), channel_id=1, source_target_pairs={{0,1},{1,0},{2,3},{3,2},{4,5},{5,4},{6,7},{7,6},{8,9},{9,8},{10,11... | collective-permute-start | bytes 3145736 | tf_op jit(solution)/shard_map/ppermute | solution.py:27
  47.5 10.6 %collective-permute-start.12 = (bf16[32,4096]{1,0:T(8,128)(2,1)S(1)}, bf16[32,4096]{1,0:T(8,128)(2,1)S(1)}, u32[]{:S(2)}, u32[]{:S(2)}) collective-permute-start(bf16[32,4096]{1,0:T(8,128)(2,1)S(1)} %shard_map.88.refs_0_), channel_id=1, source_target_pairs={{0,8},{8,0},{16,24},{24,16},{1,9},{9,1},{17,25},{25,17},{2,10},{10... | collective-permute-start | bytes 786440 | tf_op jit(solution)/shard_map/ppermute | solution.py:27
  48.5 16.3 %collective-permute-start.7 = (bf16[4,256,256]{2,1,0:T(8,128)(2,1)S(1)}, bf16[4,256,256]{2,1,0:T(8,128)(2,1)S(1)}, u32[]{:S(2)}, u32[]{:S(2)}) collective-permute-start(bf16[4,256,256]{2,1,0:T(8,128)(2,1)S(1)} %shard_map.83.refs_1_.refs_4_), channel_id=1, source_target_pairs={{0,4},{2,6},{4,0},{6,2},{1,5},{3,7},{5,1},{7,3},{8,12},{10,14},{12... | collective-permute-start | bytes 1572872 | tf_op jit(solution)/shard_map/ppermute | solution.py:27
  50.1 25.3 %collective-permute-start.6 = (bf16[4,256,256]{2,1,0:T(8,128)(2,1)S(1)}, bf16[4,256,256]{2,1,0:T(8,128)(2,1)}, u32[]{:S(2)}, u32[]{:S(2)}) collective-permute-start(bf16[4,256,256]{2,1,0:T(8,128)(2,1)S(1)} %shard_map.83.refs_1_.refs_4_), channel_id=1, source_target_pairs={{0,6},{2,4},{4,2},{6,0},{1,7},{3,5},{5,3},{7,1},{8,14},{10,12},{12... | collective-permute-start | bytes 1572872 | tf_op jit(solution)/shard_map/ppermute | solution.py:27
  51.1 25.8 %collective-permute-start.5 = (bf16[4,256,256]{2,1,0:T(8,128)(2,1)S(1)}, bf16[4,256,256]{2,1,0:T(8,128)(2,1)}, u32[]{:S(2)}, u32[]{:S(2)}) collective-permute-start(bf16[4,256,256]{2,1,0:T(8,128)(2,1)S(1)} %shard_map.83.refs_1_.refs_4_), channel_id=1, source_target_pairs={{0,2},{2,0},{4,6},{6,4},{1,3},{3,1},{5,7},{7,5},{8,10},{10,8},{12,... | collective-permute-start | bytes 1572872 | tf_op jit(solution)/shard_map/ppermute | solution.py:27
  58.2 26.9 %collective-permute-start.13 = (bf16[64,4096]{1,0:T(8,128)(2,1)S(1)}, bf16[64,4096]{1,0:T(8,128)(2,1)}, u32[]{:S(2)}, u32[]{:S(2)}) collective-permute-start(bf16[64,4096]{1,0:T(8,128)(2,1)S(1)} %shard_map.89.refs_0_), channel_id=1, source_target_pairs={{0,16},{8,24},{16,0},{24,8},{1,17},{9,25},{17,1},{25,9},{2,18},{10... | collective-permute-start | bytes 1572872 | tf_op jit(solution)/shard_map/ppermute | solution.py:27
  64.8 50.6 %collective-permute-start.22 = (bf16[1024,512]{1,0:T(8,128)(2,1)S(1)}, bf16[1024,512]{1,0:T(8,128)(2,1)S(1)}, u32[]{:S(2)}, u32[]{:S(2)}) collective-permute-start(bf16[1024,512]{1,0:T(8,128)(2,1)S(1)} %multiply_convert_fusion.refs_0_), channel_id=1, source_target_pairs={{0,64},{32,96},{64,0},{96,32},{1,65},{33,97},{65,1},{97,33},{2,66}... | collective-permute-start | bytes 3145736 | tf_op jit(solution)/shard_map/ppermute | solution.py:27
  75.4 40.0 %collective-permute-start.21 = (bf16[1024,512]{1,0:T(8,128)(2,1)S(1)}, bf16[1024,512]{1,0:T(8,128)(2,1)S(1)}, u32[]{:S(2)}, u32[]{:S(2)}) collective-permute-start(bf16[1024,512]{1,0:T(8,128)(2,1)S(1)} %multiply_convert_fusion.refs_0_), channel_id=1, source_target_pairs={{0,96},{32,64},{64,32},{96,0},{1,97},{33,65},{65,33},{97,1},{2,98}... | collective-permute-start | bytes 3145736 | tf_op jit(solution)/shard_map/ppermute | solution.py:27
  76.9 38.6 %collective-permute-start.20 = (bf16[1024,512]{1,0:T(8,128)(2,1)S(1)}, bf16[1024,512]{1,0:T(8,128)(2,1)S(1)}, u32[]{:S(2)}, u32[]{:S(2)}) collective-permute-start(bf16[1024,512]{1,0:T(8,128)(2,1)S(1)} %multiply_convert_fusion.refs_0_), channel_id=1, source_target_pairs={{0,32},{32,0},{64,96},{96,64},{1,33},{33,1},{65,97},{97,65},{2,34}... | collective-permute-start | bytes 3145736 | tf_op jit(solution)/shard_map/ppermute | solution.py:27
  78.7 6.5 %collective-permute-start.11 = (bf16[2,256,128]{2,1,0:T(8,128)(2,1)S(1)}, bf16[2,256,128]{2,1,0:T(8,128)(2,1)S(1)}, u32[]{:S(2)}, u32[]{:S(2)}) collective-permute-start(bf16[2,256,128]{2,1,0:T(8,128)(2,1)S(1)} %collective-permute-done.3.refs_2_), channel_id=1, source_target_pairs={{0,4},{2,6},{4,0},{6,2},{1,5},{3,7},{5,1},{7,3},{8,12},{10,14},{12... | collective-permute-start | bytes 393224 | tf_op jit(solution)/shard_map/ppermute | solution.py:27
  83.8 31.6 %copy-start.12 = (bf16[8,256,128]{2,1,0:T(8,128)(2,1)}, bf16[8,256,128]{2,1,0:T(8,128)(2,1)S(1)}, u32[]{:S(2)}) copy-start(bf16[8,256,128]{2,1,0:T(8,128)(2,1)S(1)} %get-tuple-element.59.refs_1_) | copy-start | bytes 1572868
  85.1 1.4 collective-permute-start.8
  85.1 7.1 %collective-permute-start.10 = (bf16[2,256,128]{2,1,0:T(8,128)(2,1)S(1)}, bf16[2,256,128]{2,1,0:T(8,128)(2,1)S(1)}, u32[]{:S(2)}, u32[]{:S(2)}) collective-permute-start(bf16[2,256,128]{2,1,0:T(8,128)(2,1)S(1)} %collective-permute-done.3.refs_2_), channel_id=1, source_target_pairs={{0,6},{2,4},{4,2},{6,0},{1,7},{3,5},{5,3},{7,1},{8,14},{10,12},{12... | collective-permute-start | bytes 393224 | tf_op jit(solution)/shard_map/ppermute | solution.py:27
  86.5 5.8 %collective-permute-start.9 = (bf16[2,256,128]{2,1,0:T(8,128)(2,1)S(1)}, bf16[2,256,128]{2,1,0:T(8,128)(2,1)S(1)}, u32[]{:S(2)}, u32[]{:S(2)}) collective-permute-start(bf16[2,256,128]{2,1,0:T(8,128)(2,1)S(1)} %collective-permute-done.3.refs_2_), channel_id=1, source_target_pairs={{0,2},{2,0},{4,6},{6,4},{1,3},{3,1},{5,7},{7,5},{8,10},{10,8},{12,... | collective-permute-start | bytes 393224 | tf_op jit(solution)/shard_map/ppermute | solution.py:27
  87.8 31.6 %copy-start.16 = (bf16[64,4096]{1,0:T(8,128)(2,1)}, bf16[64,4096]{1,0:T(8,128)(2,1)S(1)}, u32[]{:S(2)}) copy-start(bf16[64,4096]{1,0:T(8,128)(2,1)S(1)} %get-tuple-element.54.refs_0_) | copy-start | bytes 1572868
  92.3 23.2 %copy-start.22 = (bf16[2,256,128]{2,1,0:T(8,128)(2,1)}, bf16[2,256,128]{2,1,0:T(8,128)(2,1)S(1)}, u32[]{:S(2)}) copy-start(bf16[2,256,128]{2,1,0:T(8,128)(2,1)S(1)} %collective-permute-done.10.refs_4_) | copy-start | bytes 393220
  92.3 23.2 %copy-start.24 = (bf16[2,256,128]{2,1,0:T(8,128)(2,1)}, bf16[2,256,128]{2,1,0:T(8,128)(2,1)S(1)}, u32[]{:S(2)}) copy-start(bf16[2,256,128]{2,1,0:T(8,128)(2,1)S(1)} %collective-permute-done.9.refs_3_) | copy-start | bytes 393220
  115.5 34.8 %copy-start.13 = (bf16[8,256,128]{2,1,0:T(8,128)(2,1)S(1)}, bf16[8,256,128]{2,1,0:T(8,128)(2,1)}, u32[]{:S(2)}) copy-start(bf16[8,256,128]{2,1,0:T(8,128)(2,1)} %copy-done.12) | copy-start | bytes 1572868
  115.5 34.8 %copy-start.23 = (bf16[2,256,128]{2,1,0:T(8,128)(2,1)S(1)}, bf16[2,256,128]{2,1,0:T(8,128)(2,1)}, u32[]{:S(2)}) copy-start(bf16[2,256,128]{2,1,0:T(8,128)(2,1)} %copy-done.22) | copy-start | bytes 393220
  115.5 34.8 %copy-start.25 = (bf16[2,256,128]{2,1,0:T(8,128)(2,1)S(1)}, bf16[2,256,128]{2,1,0:T(8,128)(2,1)}, u32[]{:S(2)}) copy-start(bf16[2,256,128]{2,1,0:T(8,128)(2,1)} %copy-done.24) | copy-start | bytes 393220
  117.7 32.5 %collective-permute-start.23 = (bf16[4096,512]{1,0:T(8,128)(2,1)}, bf16[4096,512]{1,0:T(8,128)(2,1)}, u32[]{:S(2)}, u32[]{:S(2)}) collective-permute-start(bf16[4096,512]{1,0:T(8,128)(2,1)} %shard_map.92.refs_6_.refs_4_), channel_id=1, source_target_pairs={{0,1},{1,0},{2,3},{3,2},{4,5},{5,4},{6,7},{7,6},{8,9},{9,8},{10,11... | collective-permute-start | bytes 12582920 | tf_op jit(solution)/shard_map/ppermute | solution.py:27
  117.7 16.0 %collective-permute-start.15 = (bf16[64,4096]{1,0:T(8,128)(2,1)S(1)}, bf16[64,4096]{1,0:T(8,128)(2,1)}, u32[]{:S(2)}, u32[]{:S(2)}) collective-permute-start(bf16[64,4096]{1,0:T(8,128)(2,1)S(1)} %get-tuple-element.54.refs_0_), channel_id=1, source_target_pairs={{0,6},{2,4},{4,2},{6,0},{1,7},{3,5},{5,3},{7,1},{8,14},{10,12},{12... | collective-permute-start | bytes 1572872 | tf_op jit(solution)/shard_map/ppermute | solution.py:27
  118.6 15.2 %collective-permute-start.16 = (bf16[64,4096]{1,0:T(8,128)(2,1)S(1)}, bf16[64,4096]{1,0:T(8,128)(2,1)S(1)}, u32[]{:S(2)}, u32[]{:S(2)}) collective-permute-start(bf16[64,4096]{1,0:T(8,128)(2,1)S(1)} %get-tuple-element.55.refs_0_), channel_id=1, source_target_pairs={{0,2},{2,0},{4,6},{6,4},{1,3},{3,1},{5,7},{7,5},{8,10},{10,8},{12,... | collective-permute-start | bytes 1572872 | tf_op jit(solution)/shard_map/ppermute | solution.py:27
  119.4 25.2 %collective-permute-start.14 = (bf16[64,4096]{1,0:T(8,128)(2,1)S(1)}, bf16[64,4096]{1,0:T(8,128)(2,1)S(1)}, u32[]{:S(2)}, u32[]{:S(2)}) collective-permute-start(bf16[64,4096]{1,0:T(8,128)(2,1)S(1)} %get-tuple-element.54.refs_0_), channel_id=1, source_target_pairs={{0,2},{2,0},{4,6},{6,4},{1,3},{3,1},{5,7},{7,5},{8,10},{10,8},{12,... | collective-permute-start | bytes 1572872 | tf_op jit(solution)/shard_map/ppermute | solution.py:27
  120.6 24.8 %collective-permute-start.17 = (bf16[64,4096]{1,0:T(8,128)(2,1)S(1)}, bf16[64,4096]{1,0:T(8,128)(2,1)S(1)}, u32[]{:S(2)}, u32[]{:S(2)}) collective-permute-start(bf16[64,4096]{1,0:T(8,128)(2,1)S(1)} %get-tuple-element.55.refs_0_), channel_id=1, source_target_pairs={{0,6},{2,4},{4,2},{6,0},{1,7},{3,5},{5,3},{7,1},{8,14},{10,12},{12... | collective-permute-start | bytes 1572872 | tf_op jit(solution)/shard_map/ppermute | solution.py:27
  133.8 24.7 %collective-permute-start.18 = (bf16[64,4096]{1,0:T(8,128)(2,1)}, bf16[64,4096]{1,0:T(8,128)(2,1)}, u32[]{:S(2)}, u32[]{:S(2)}) collective-permute-start(bf16[64,4096]{1,0:T(8,128)(2,1)} %collective-permute-done.15.refs_2_), channel_id=1, source_target_pairs={{0,2},{2,0},{4,6},{6,4},{1,3},{3,1},{5,7},{7,5},{8,10},{10,8},{12,... | collective-permute-start | bytes 1572872 | tf_op jit(solution)/shard_map/ppermute | solution.py:27
  133.8 22.0 %copy-start.6 = (bf16[64,4096]{1,0:T(8,128)(2,1)}, bf16[64,4096]{1,0:T(8,128)(2,1)S(1)}, u32[]{:S(2)}) copy-start(bf16[64,4096]{1,0:T(8,128)(2,1)S(1)} %collective-permute-done.16.refs_1_) | copy-start | bytes 1572868
  133.8 24.7 %collective-permute-start.19 = (bf16[64,4096]{1,0:T(8,128)(2,1)S(1)}, bf16[64,4096]{1,0:T(8,128)(2,1)S(1)}, u32[]{:S(2)}, u32[]{:S(2)}) collective-permute-start(bf16[64,4096]{1,0:T(8,128)(2,1)S(1)} %collective-permute-done.16.refs_1_), channel_id=1, source_target_pairs={{0,6},{2,4},{4,2},{6,0},{1,7},{3,5},{5,3},{7,1},{8,14},{10,12},{12... | collective-permute-start | bytes 1572872 | tf_op jit(solution)/shard_map/ppermute | solution.py:27
  146.2 12.3 %all-to-all-start.3 = ((bf16[4,32,1024]{2,1,0:T(8,128)(2,1)}), bf16[4,32,1024]{2,1,0:T(8,128)(2,1)}, u32[]{:S(2)}, u32[]{:S(2)}) async-start(bf16[4,32,1024]{2,1,0:T(8,128)(2,1)} %broadcast_in_dim.18), calls=%async_computation.3 | async-start | bytes 524288 | tf_op jit(solution)/shard_map/all_to_all | solution.py:47
  155.8 14.8 %copy-start.17 = (bf16[64,4096]{1,0:T(8,128)(2,1)S(1)}, bf16[64,4096]{1,0:T(8,128)(2,1)}, u32[]{:S(2)}) copy-start(bf16[64,4096]{1,0:T(8,128)(2,1)} %copy-done.16) | copy-start | bytes 1572868
  155.8 9.2 %collective-permute-start.24 = (bf16[128,1024]{1,0:T(8,128)(2,1)}, bf16[128,1024]{1,0:T(8,128)(2,1)S(1)}, u32[]{:S(2)}, u32[]{:S(2)}) collective-permute-start(bf16[128,1024]{1,0:T(8,128)(2,1)} %get-tuple-element.66), channel_id=1, source_target_pairs={{0,1},{1,0},{2,3},{3,2},{4,5},{5,4},{6,7},{7,6},{8,9},{9,8},{10,11... | collective-permute-start | bytes 786440 | tf_op jit(solution)/shard_map/ppermute | solution.py:27
  160.7 17.7 %all-to-all-start.4 = ((bf16[4,4,32,1024]{3,2,1,0:T(8,128)(2,1)}), bf16[4,4,32,1024]{3,2,1,0:T(8,128)(2,1)}, u32[]{:S(2)}, u32[]{:S(2)}) async-start(bf16[4,4,32,1024]{3,2,1,0:T(8,128)(2,1)} %broadcast_in_dim.19), calls=%async_computation.4 | async-start | bytes 2097152 | tf_op jit(solution)/shard_map/all_to_all | solution.py:47
  165.1 12.6 %collective-permute-start.25 = (bf16[128,1024]{1,0:T(8,128)(2,1)S(1)}, bf16[128,1024]{1,0:T(8,128)(2,1)S(1)}, u32[]{:S(2)}, u32[]{:S(2)}) collective-permute-start(bf16[128,1024]{1,0:T(8,128)(2,1)S(1)} %fusion.3), channel_id=1, source_target_pairs={{0,128},{128,0},{1,129},{129,1},{2,130},{130,2},{3,131},{131,3},{4... | collective-permute-start | bytes 786440 | tf_op jit(solution)/shard_map/ppermute | solution.py:27
  178.4 10.6 %collective-permute-start.26 = (bf16[512,1024]{1,0:T(8,128)(2,1)}, bf16[512,1024]{1,0:T(8,128)(2,1)}, u32[]{:S(2)}, u32[]{:S(2)}) collective-permute-start(bf16[512,1024]{1,0:T(8,128)(2,1)} %bitcast.16), channel_id=1, source_target_pairs={{0,1},{1,0},{2,3},{3,2},{4,5},{5,4},{6,7},{7,6},{8,9},{9,8},{10,11... | collective-permute-start | bytes 3145736 | tf_op jit(solution)/shard_map/ppermute | solution.py:27
  178.8 18.5 %collective-permute-start.27 = (bf16[256,1024]{1,0:T(8,128)(2,1)S(1)}, bf16[256,1024]{1,0:T(8,128)(2,1)S(1)}, u32[]{:S(2)}, u32[]{:S(2)}) collective-permute-start(bf16[256,1024]{1,0:T(8,128)(2,1)S(1)} %shard_map.94), channel_id=1, source_target_pairs={{0,128},{128,0},{1,129},{129,1},{2,130},{130,2},{3,131},{131,3},{4... | collective-permute-start | bytes 1572872 | tf_op jit(solution)/shard_map/ppermute | solution.py:27
  184.3 13.0 %collective-permute-start.30 = (bf16[128,1024]{1,0:T(8,128)(2,1)S(1)}, bf16[128,1024]{1,0:T(8,128)(2,1)S(1)}, u32[]{:S(2)}, u32[]{:S(2)}) collective-permute-start(bf16[128,1024]{1,0:T(8,128)(2,1)S(1)} %add_convert_fusion.1.refs_0_), channel_id=1, source_target_pairs={{0,64},{32,96},{64,0},{96,32},{1,65},{33,97},{65,1},{97,33},{2,66}... | collective-permute-start | bytes 786440 | tf_op jit(solution)/shard_map/ppermute | solution.py:27
  186.3 13.5 %collective-permute-start.29 = (bf16[128,1024]{1,0:T(8,128)(2,1)S(1)}, bf16[128,1024]{1,0:T(8,128)(2,1)S(1)}, u32[]{:S(2)}, u32[]{:S(2)}) collective-permute-start(bf16[128,1024]{1,0:T(8,128)(2,1)S(1)} %add_convert_fusion.1.refs_0_), channel_id=1, source_target_pairs={{0,96},{32,64},{64,32},{96,0},{1,97},{33,65},{65,33},{97,1},{2,98}... | collective-permute-start | bytes 786440 | tf_op jit(solution)/shard_map/ppermute | solution.py:27
  188.8 11.0 %collective-permute-start.28 = (bf16[128,1024]{1,0:T(8,128)(2,1)S(1)}, bf16[128,1024]{1,0:T(8,128)(2,1)S(1)}, u32[]{:S(2)}, u32[]{:S(2)}) collective-permute-start(bf16[128,1024]{1,0:T(8,128)(2,1)S(1)} %add_convert_fusion.1.refs_0_), channel_id=1, source_target_pairs={{0,32},{32,0},{64,96},{96,64},{1,33},{33,1},{65,97},{97,65},{2,34}... | collective-permute-start | bytes 786440 | tf_op jit(solution)/shard_map/ppermute | solution.py:27
  200.8 32.2 %all-to-all-start.5 = ((bf16[16,16,1152]{2,1,0:T(8,128)(2,1)}), bf16[16,16,1152]{2,1,0:T(8,128)(2,1)S(1)}, u32[]{:S(2)}, u32[]{:S(2)}) async-start(bf16[16,16,1152]{2,1,0:T(8,128)(2,1)} %broadcast_in_dim.20), calls=%async_computation.5 | async-start | bytes 1179648 | tf_op jit(solution)/shard_map/all_to_all | solution.py:47
  217.3 9.0 %collective-permute-start.31 = (bf16[512,1024]{1,0:T(8,128)(2,1)S(1)}, bf16[512,1024]{1,0:T(8,128)(2,1)S(1)}, u32[]{:S(2)}, u32[]{:S(2)}) collective-permute-start(bf16[512,1024]{1,0:T(8,128)(2,1)S(1)} %shard_map.96.refs_2_), channel_id=1, source_target_pairs={{0,1},{1,0},{2,3},{3,2},{4,5},{5,4},{6,7},{7,6},{8,9},{9,8},{10,11... | collective-permute-start | bytes 3145736 | tf_op jit(solution)/shard_map/ppermute | solution.py:27
  (19 other events, 48.9 us)
where the time goes:
time: 253 us; the launch traced here: 251 us
  starting transfers between devices  87.4 us (35%)
  waiting for transfers between devices  66.8 us (26%)
  blocking collectives  36.5 us (14%)
  Pallas kernels  33.5 us (13%)
  local copies, waits for them, and re-layouts  18.6 us (7%)
  matrix products  4.99 us (2%)
  other arithmetic  2.9 us (1%)
    ppermute x32, waiting for transfers between devices, hop(): return lax.ppermute(block, axis, [(i, i ^ bit) for i in range(size)])  49.6 us
    ppermute x32, starting transfers between devices, hop(): return lax.ppermute(block, axis, [(i, i ^ bit) for i in range(size)])  47.6 us
    pallas_call x18, Pallas kernels, kernel_call(): pl.pallas_call(inner, out_shape=shapes, in_specs=[small] * len(scalars) +...  33.5 us
    all_to_all x3, starting transfers between devices, spread(): return lax.all_to_all(copies, axis, 0, 0, tiled=True)  23.8 us
    all_to_all x1, blocking collectives, per_device(): incoming = lax.all_to_all(outgoing, SECTION, 0, 0, tiled=True)  23.1 us
    all_to_all x1, blocking collectives, per_device(): sums = lax.all_to_all(sums, PLANE, 0, 0, tiled=True)  13.4 us
    unnamed x61, local copies, waits for them, and re-layouts  13 us
    all_to_all x3, waiting for transfers between devices, spread(): return lax.all_to_all(copies, axis, 0, 0, tiled=True)  8.93 us
  transfers between devices with their start and end apart: 37, of which 15 were waited for; matrix products, arithmetic and copies ran while one was open for 4% of the time, Pallas kernels for 11%

commit v1 on v0

--- a/solution.py
+++ b/solution.py
@@ -242,8 +242,22 @@
         )
 
 
-def chain_kernel(where_ref, products_ref, gram_ref, square_ref, sent_ref, latent_ref):
+def chain_kernel(
+    where_ref, products_ref, own_ref, other_ref, square_ref, sent_ref, latent_ref, gram_ref
+):
     layers, each, rank = products_ref.shape
+    half = own_ref.shape[0]
+
+    @pl.when(where_ref[4] == 0)
+    def _():
+        gram_ref[:half] = own_ref[...]
+        gram_ref[half:] = other_ref[...]
+
+    @pl.when(where_ref[4] != 0)
+    def _():
+        gram_ref[:half] = other_ref[...]
+        gram_ref[half:] = own_ref[...]
+
     rows = each // 4
     width = where_ref[6].astype(F32)
     square = square_ref[...]
@@ -445,7 +459,7 @@
     )
     gram = spread(tied(gram, *passing[1:3], *staying[1:3]), "zlo")
     gram = spread(tied(gram, passing[3], staying[3]), "y").reshape(-1, sections * rank)
-    head = stack([tied(piece, incoming) for piece in head_pieces])
+    head = stack([tied(piece, outgoing) for piece in head_pieces])
     other_head = hop(head, "core", 1)
     wide = 2 * head_columns
     mine, theirs = kernel_call(
@@ -472,19 +486,19 @@
     steps = jnp.arange(4, dtype=jnp.int32)
     at = ((steps[None, :] * 4 + steps[:, None]) * own_rank)[..., None, None]
     at = at + (steps * rank)[:, None] + jnp.arange(own_rank, dtype=jnp.int32)
-    at = at.reshape(-1)
-    line = jnp.arange(sections * rank, dtype=jnp.int32)[:, None]
-    own_sorting = (line == (at + core * 4 * rank)[None, :]).astype(BF16)
-    other_sorting = (line == (at + (1 - core) * 4 * rank)[None, :]).astype(BF16)
-    gram = jnp.dot(own_sorting, gram, preferred_element_type=F32) + jnp.dot(
-        other_sorting, hop(gram, "core", 1), preferred_element_type=F32
-    )
+    line = jnp.arange(4 * rank, dtype=jnp.int32)[:, None]
+    sorting = (line == at.reshape(1, -1)).astype(BF16)
+    gram = jnp.dot(sorting, gram, preferred_element_type=F32).astype(BF16)
+    partner_gram = hop(gram, "core", 1)
     (latents,) = kernel_call(
         chain_kernel,
         [((rows, (sections + 1) * rank), BF16, "v")],
         [where],
-        [incoming, gram.astype(BF16), own_square],
-        scratch=[pltpu.VMEM((rows, sections * rank), BF16)],
+        [incoming, gram, partner_gram, own_square],
+        scratch=[
+            pltpu.VMEM((rows, sections * rank), BF16),
+            pltpu.VMEM((sections * rank, sections * rank), BF16),
+        ],
     )
 
     latents = spread(tied(latents, passed, *correction), PLANE)

time: 253 us -> 249 us (0.984)
  blocking collectives: 36.5 us -> 13.4 us
  waiting for transfers between devices: 66.8 us -> 83.1 us
  starting transfers between devices: 87.4 us -> 95.2 us
  matrix products: 4.99 us -> 1.94 us
    all_to_all x1 -> x0, blocking collectives: 23.1 us -> none  [per_device(): incoming = lax.all_to_all(outgoing, SECTION, 0, 0, tiled=True)]
    ppermute x32, waiting for transfers between devices: 49.6 us -> 59 us  [hop(): return lax.ppermute(block, axis, [(i, i ^ bit) for i in range(size)])]
    all_to_all x0 -> x1, starting transfers between devices: none -> 9.3 us  [per_device(): incoming = lax.all_to_all(outgoing, SECTION, 0, 0, tiled=True)]
    all_to_all x0 -> x1, waiting for transfers between devices: none -> 6.33 us  [per_device(): incoming = lax.all_to_all(outgoing, SECTION, 0, 0, tiled=True)]
    dot_general x2 -> x1, matrix products: 4.99 us -> 1.94 us  [per_device(): gram = jnp.dot(sorting, gram, preferred_element_type=F32).astype(BF16)]
    unnamed x61 -> x51, local copies, waits for them, and re-layouts: 13 us -> 11.6 us
  transfers between devices with their start and end apart: 37 -> 38, of which waited for: 15 -> 17; matrix products, arithmetic and copies ran while one was open for 4% -> 2% of each run, Pallas kernels for 11% -> 12%
where the time goes in v1:
time: 249 us; the launch traced here: 248 us
  starting transfers between devices  95.2 us (38%)
  waiting for transfers between devices  83.1 us (33%)
  Pallas kernels  35.5 us (14%)
  local copies, waits for them, and re-layouts  16.3 us (7%)
  blocking collectives  13.4 us (5%)
    ppermute x32, waiting for transfers between devices, hop(): return lax.ppermute(block, axis, [(i, i ^ bit) for i in range(size)])  59 us
    ppermute x32, starting transfers between devices, hop(): return lax.ppermute(block, axis, [(i, i ^ bit) for i in range(size)])  45.5 us
    pallas_call x18, Pallas kernels, kernel_call(): pl.pallas_call(inner, out_shape=shapes, in_specs=[small] * len(scalars) +...  35.5 us
    all_to_all x3, starting transfers between devices, spread(): return lax.all_to_all(copies, axis, 0, 0, tiled=True)  24.4 us
    all_to_all x1, blocking collectives, per_device(): sums = lax.all_to_all(sums, PLANE, 0, 0, tiled=True)  13.4 us
    unnamed x51, local copies, waits for them, and re-layouts  11.6 us
    all_to_all x3, waiting for transfers between devices, spread(): return lax.all_to_all(copies, axis, 0, 0, tiled=True)  9.53 us
    all_to_all x1, starting transfers between devices, per_device(): incoming = lax.all_to_all(outgoing, SECTION, 0, 0, tiled=True)  9.3 us
  transfers between devices with their start and end apart: 38, of which 17 were waited for; matrix products, arithmetic and copies ran while one was open for 2% of the time, Pallas kernels for 12%

profile of v1, /device:TPU:2, one launch (start us, length us, event | category | flops | bytes accessed | tf_op | source)
XLA Modules:
  0.0 247.6 jit_solution(6595520861862995275)
XLA Ops:
  2.0 4.7 %collective-permute-start.2 = (bf16[256,256]{1,0:T(8,128)(2,1)S(1)}, bf16[256,256]{1,0:T(8,128)(2,1)S(1)}, u32[]{:S(2)}, u32[]{:S(2)}) collective-permute-start(bf16[256,256]{1,0:T(8,128)(2,1)S(1)} %pad_maximum_fusion), channel_id=1, source_target_pairs={{0,24},{8,16},{16,8},{24,0},{1,25},{9,17},{17,9},{25,1},{2,26},{10... | collective-permute-start | bytes 393224 | tf_op jit(solution)/shard_map/ppermute | solution.py:27
  7.4 7.7 %all-to-all-start = ((bf16[16,8,256]{2,1,0:T(8,128)(2,1)}), bf16[16,8,256]{2,1,0:T(8,128)(2,1)S(1)}, u32[]{:S(2)}, u32[]{:S(2)}) async-start(bf16[16,8,256]{2,1,0:T(8,128)(2,1)} %bitcast.26), calls=%async_computation | async-start | bytes 131072 | tf_op jit(solution)/shard_map/all_to_all | solution.py:391
  15.2 8.3 %all-to-all-done.refs_1_ = bf16[16,8,256]{2,1,0:T(8,128)(2,1)S(1)} async-done(((bf16[16,8,256]{2,1,0:T(8,128)(2,1)}), bf16[16,8,256]{2,1,0:T(8,128)(2,1)S(1)}, u32[]{:S(2)}, u32[]{:S(2)}) %all-to-all-start) | async-done | bytes 65568 | tf_op jit(solution)/shard_map/all_to_all | solution.py:391
  24.2 4.6 %collective-permute-start.3 = (bf16[2,256,128]{2,1,0:T(8,128)(2,1)S(1)}, bf16[2,256,128]{2,1,0:T(8,128)(2,1)S(1)}, u32[]{:S(2)}, u32[]{:S(2)}) collective-permute-start(bf16[2,256,128]{2,1,0:T(8,128)(2,1)S(1)} %shard_map.84), channel_id=1, source_target_pairs={{0,128},{128,0},{1,129},{129,1},{2,130},{130,2},{3,131},{131,3},{4... | collective-permute-start | bytes 393224 | tf_op jit(solution)/shard_map/ppermute | solution.py:27
  28.7 1.4 shard_map.85
  30.1 3.9 %collective-permute-done.3.refs_2_ = bf16[2,256,128]{2,1,0:T(8,128)(2,1)S(1)} collective-permute-done((bf16[2,256,128]{2,1,0:T(8,128)(2,1)S(1)}, bf16[2,256,128]{2,1,0:T(8,128)(2,1)S(1)}, u32[]{:S(2)}, u32[]{:S(2)}) %collective-permute-start.3) | collective-permute-done | bytes 131104 | tf_op jit(solution)/shard_map/ppermute | solution.py:27
  34.0 8.3 %all-to-all-start.1 = ((bf16[8,8,4096]{2,1,0:T(8,128)(2,1)}), bf16[8,8,4096]{2,1,0:T(8,128)(2,1)S(1)}, u32[]{:S(2)}, u32[]{:S(2)}) async-start(bf16[8,8,4096]{2,1,0:T(8,128)(2,1)} %shard_map.85), calls=%async_computation.1 | async-start | bytes 1048576 | tf_op jit(solution)/shard_map/all_to_all | solution.py:435
  43.5 1.9 collective-permute-start.6
  45.4 1.6 copy-done.1
  47.0 2.9 %shard_map.82 = (bf16[128,4096]{1,0:T(8,128)(2,1)S(1)}, bf16[128,4096]{1,0:T(8,128)(2,1)}, f32[16,1]{1,0:T(8,128)S(1)}, bf16[128,8192]{1,0:T(8,128)(2,1)S(1)}, s32[256,1]{1,0:T(8,128)S(1)}, /*index=5*/s32[32]{0:T(128)}) custom-call(s32[7]{0:T(128)S(1)} %stack.27.refs_0_, s32[32]{0:T(128)S(1)} %copy-done.23, bf16[32,4,8192]{2,1,0:T(4,128)(2,1)S(1)} %copy-done.1, ...), custom_call_target="tpu_custom_call" | custom-call | tf_op jit(solution)/shard_map/pallas_call | solution.py:66
  53.8 7.3 %collective-permute-done.12.refs_1_ = bf16[32,4096]{1,0:T(8,128)(2,1)} collective-permute-done((bf16[32,4096]{1,0:T(8,128)(2,1)S(1)}, bf16[32,4096]{1,0:T(8,128)(2,1)}, u32[]{:S(2)}, u32[]{:S(2)}) %collective-permute-start.12) | collective-permute-done | bytes 262176 | tf_op jit(solution)/shard_map/ppermute | solution.py:27
  61.1 2.1 collective-permute-start.22
  63.2 1.5 collective-permute-done.6.refs_6_
  66.8 2.1 collective-permute-start.13
  69.0 1.5 collective-permute-start.11
  70.5 2.6 %shard_map.86 = (f32[288,128]{1,0:T(8,128)S(1)}, f32[288,128]{1,0:T(8,128)S(1)}, bf16[8,256,128]{2,1,0:T(8,128)(2,1)S(1)}) custom-call(s32[7]{0:T(128)S(1)} %stack.27.refs_0_, bf16[128,4096]{1,0:T(8,128)(2,1)S(1)} %copy-done.3, bf16[128,4096]{1,0:T(8,128)(2,1)} %collective-permute-done.4.refs_2_, bf16[64,4096]{1,0:T(8,128)(2,1)S(1)} %bitcast.21, ...), custom_call_target="tpu_custom_call" | custom-call | tf_op jit(solution)/shard_map/pallas_call | solution.py:66
  73.1 2.6 %collective-permute-done.11.refs_5_ = bf16[2,256,128]{2,1,0:T(8,128)(2,1)S(1)} collective-permute-done((bf16[2,256,128]{2,1,0:T(8,128)(2,1)}, bf16[2,256,128]{2,1,0:T(8,128)(2,1)S(1)}, u32[]{:S(2)}, u32[]{:S(2)}) %collective-permute-start.11) | collective-permute-done | bytes 131104 | tf_op jit(solution)/shard_map/ppermute | solution.py:27
  75.7 16.7 %collective-permute-done.13.refs_1_ = bf16[64,4096]{1,0:T(8,128)(2,1)S(1)} collective-permute-done((bf16[64,4096]{1,0:T(8,128)(2,1)S(1)}, bf16[64,4096]{1,0:T(8,128)(2,1)S(1)}, u32[]{:S(2)}, u32[]{:S(2)}) %collective-permute-start.13) | collective-permute-done | bytes 524320 | tf_op jit(solution)/shard_map/ppermute | solution.py:27
  92.3 1.3 collective-permute-start.10
  95.4 3.1 %collective-permute-done.10.refs_4_ = bf16[2,256,128]{2,1,0:T(8,128)(2,1)S(1)} collective-permute-done((bf16[2,256,128]{2,1,0:T(8,128)(2,1)S(1)}, bf16[2,256,128]{2,1,0:T(8,128)(2,1)S(1)}, u32[]{:S(2)}, u32[]{:S(2)}) %collective-permute-start.10) | collective-permute-done | bytes 131104 | tf_op jit(solution)/shard_map/ppermute | solution.py:27
  98.7 10.9 %collective-permute-done.21.refs_2_ = bf16[1024,512]{1,0:T(8,128)(2,1)S(1)} collective-permute-done((bf16[1024,512]{1,0:T(8,128)(2,1)S(1)}, bf16[1024,512]{1,0:T(8,128)(2,1)S(1)}, u32[]{:S(2)}, u32[]{:S(2)}) %collective-permute-start.21) | collective-permute-done | bytes 1048608 | tf_op jit(solution)/shard_map/ppermute | solution.py:27
  109.6 2.3 shard_map.92.refs_6_.refs_4_
  111.9 1.6 collective-permute-start.15
  115.6 1.6 collective-permute-start.17
  117.2 9.3 %all-to-all-start.2 = ((f32[8,64,128]{2,1,0:T(8,128)}), f32[8,64,128]{2,1,0:T(8,128)S(1)}, u32[]{:S(2)}, u32[]{:S(2)}) async-start(f32[8,64,128]{2,1,0:T(8,128)} %shard_map.87), calls=%async_computation.2 | async-start | bytes 524288 | tf_op jit(solution)/shard_map/all_to_all | solution.py:456
  126.5 1.7 collective-permute-done.15.refs_2_
  128.6 1.3 collective-permute-start.19
  129.9 6.3 %all-to-all-done.2.refs_0_.refs_1_ = f32[8,64,128]{2,1,0:T(8,128)S(1)} async-done(((f32[8,64,128]{2,1,0:T(8,128)}), f32[8,64,128]{2,1,0:T(8,128)S(1)}, u32[]{:S(2)}, u32[]{:S(2)}) %all-to-all-start.2) | async-done | bytes 262176 | tf_op jit(solution)/shard_map/all_to_all | solution.py:456
  136.3 3.4 %collective-permute-done.14.refs_1_ = bf16[64,4096]{1,0:T(8,128)(2,1)} collective-permute-done((bf16[64,4096]{1,0:T(8,128)(2,1)}, bf16[64,4096]{1,0:T(8,128)(2,1)}, u32[]{:S(2)}, u32[]{:S(2)}) %collective-permute-start.14) | collective-permute-done | bytes 524320 | tf_op jit(solution)/shard_map/ppermute | solution.py:27
  140.4 4.0 %all-to-all-start.3 = ((bf16[4,32,1024]{2,1,0:T(8,128)(2,1)}), bf16[4,32,1024]{2,1,0:T(8,128)(2,1)}, u32[]{:S(2)}, u32[]{:S(2)}) async-start(bf16[4,32,1024]{2,1,0:T(8,128)(2,1)} %broadcast_in_dim.18), calls=%async_computation.3 | async-start | bytes 524288 | tf_op jit(solution)/shard_map/all_to_all | solution.py:47
  144.5 5.5 %shard_map.93 = (f32[128,1024]{1,0:T(8,128)S(1)}, bf16[128,1024]{1,0:T(8,128)(2,1)}) custom-call(s32[7]{0:T(128)S(1)} %stack.27.refs_0_, bf16[8,256,128]{2,1,0:T(8,128)(2,1)S(1)} %copy-done.13, bf16[2,256,128]{2,1,0:T(8,128)(2,1)S(1)} %copy-done.19, bf16[2,256,128]{2,1,0:T(8,128)(2,1)S(1)} %collective-permute-done.9.refs_3_, ...), custom_call_target="tpu_custom_call" | custom-call | tf_op jit(solution)/shard_map/pallas_call | solution.py:66
  150.0 2.9 %all-to-all-done.3 = bf16[4,32,1024]{2,1,0:T(8,128)(2,1)} async-done(((bf16[4,32,1024]{2,1,0:T(8,128)(2,1)}), bf16[4,32,1024]{2,1,0:T(8,128)(2,1)}, u32[]{:S(2)}, u32[]{:S(2)}) %all-to-all-start.3) | async-done | bytes 262176 | tf_op jit(solution)/shard_map/all_to_all | solution.py:47
  152.9 2.2 broadcast_in_dim.19
  155.1 4.3 %all-to-all-start.4 = ((bf16[4,4,32,1024]{3,2,1,0:T(8,128)(2,1)}), bf16[4,4,32,1024]{3,2,1,0:T(8,128)(2,1)}, u32[]{:S(2)}, u32[]{:S(2)}) async-start(bf16[4,4,32,1024]{3,2,1,0:T(8,128)(2,1)} %broadcast_in_dim.19), calls=%async_computation.4 | async-start | bytes 2097152 | tf_op jit(solution)/shard_map/all_to_all | solution.py:47
  159.5 5.4 %collective-permute-start.25 = (bf16[128,1024]{1,0:T(8,128)(2,1)S(1)}, bf16[128,1024]{1,0:T(8,128)(2,1)S(1)}, u32[]{:S(2)}, u32[]{:S(2)}) collective-permute-start(bf16[128,1024]{1,0:T(8,128)(2,1)S(1)} %fusion.1), channel_id=1, source_target_pairs={{0,128},{128,0},{1,129},{129,1},{2,130},{130,2},{3,131},{131,3},{4... | collective-permute-start | bytes 786440 | tf_op jit(solution)/shard_map/ppermute | solution.py:27
  165.1 6.4 %shard_map.94 = bf16[256,1024]{1,0:T(8,128)(2,1)S(1)} custom-call(bf16[64,4096]{1,0:T(8,128)(2,1)} %get-tuple-element.54.refs_0_, bf16[64,4096]{1,0:T(8,128)(2,1)} %collective-permute-done.14.refs_1_, bf16[64,4096]{1,0:T(8,128)(2,1)} %collective-permute-done.15.refs_2_, bf16[64,4096]{1,0:T(8,128)(2,1)} %collective-permute-done.18.refs_3_, ...), custom_call_target="tpu_custom_call" | custom-call | tf_op jit(solution)/shard_map/pallas_call | solution.py:66
  172.6 1.9 convolution_convert_fusion.refs_2_
  174.7 5.5 %collective-permute-start.27 = (bf16[256,1024]{1,0:T(8,128)(2,1)S(1)}, bf16[256,1024]{1,0:T(8,128)(2,1)S(1)}, u32[]{:S(2)}, u32[]{:S(2)}) collective-permute-start(bf16[256,1024]{1,0:T(8,128)(2,1)S(1)} %shard_map.94), channel_id=1, source_target_pairs={{0,128},{128,0},{1,129},{129,1},{2,130},{130,2},{3,131},{131,3},{4... | collective-permute-start | bytes 1572872 | tf_op jit(solution)/shard_map/ppermute | solution.py:27
  180.1 2.0 collective-permute-start.30
  182.2 2.7 %collective-permute-start.28 = (bf16[128,1024]{1,0:T(8,128)(2,1)S(1)}, bf16[128,1024]{1,0:T(8,128)(2,1)S(1)}, u32[]{:S(2)}, u32[]{:S(2)}) collective-permute-start(bf16[128,1024]{1,0:T(8,128)(2,1)S(1)} %add_convert_fusion.refs_0_), channel_id=1, source_target_pairs={{0,32},{32,0},{64,96},{96,64},{1,33},{33,1},{65,97},{97,65},{2,34}... | collective-permute-start | bytes 786440 | tf_op jit(solution)/shard_map/ppermute | solution.py:27
  184.8 3.1 %shard_map.95 = bf16[16,1152]{1,0:T(8,128)(2,1)S(1)} custom-call(s32[7]{0:T(128)S(1)} %stack.27.refs_0_, f32[8,64,128]{2,1,0:T(8,128)S(1)} %all-to-all-done.2.refs_0_.refs_1_, bf16[512,1024]{1,0:T(8,128)(2,1)S(1)} %convolution_convert_fusion.refs_2_, bf16[512,1024]{1,0:T(8,128)(2,1)S(1)} %collective-permute-done.26.refs_3_, ...), custom_call_target="tpu_custom_call" | custom-call | tf_op jit(solution)/shard_map/pallas_call | solution.py:66
  187.9 5.2 %collective-permute-done.27.refs_5_ = bf16[256,1024]{1,0:T(8,128)(2,1)S(1)} collective-permute-done((bf16[256,1024]{1,0:T(8,128)(2,1)S(1)}, bf16[256,1024]{1,0:T(8,128)(2,1)S(1)}, u32[]{:S(2)}, u32[]{:S(2)}) %collective-permute-start.27) | collective-permute-done | bytes 524320 | tf_op jit(solution)/shard_map/ppermute | solution.py:27
  193.1 2.5 %collective-permute-done.29.refs_2_ = bf16[128,1024]{1,0:T(8,128)(2,1)S(1)} collective-permute-done((bf16[128,1024]{1,0:T(8,128)(2,1)S(1)}, bf16[128,1024]{1,0:T(8,128)(2,1)S(1)}, u32[]{:S(2)}, u32[]{:S(2)}) %collective-permute-start.29) | collective-permute-done | bytes 262176 | tf_op jit(solution)/shard_map/ppermute | solution.py:27
  196.5 16.1 %all-to-all-start.5 = ((bf16[16,16,1152]{2,1,0:T(8,128)(2,1)}), bf16[16,16,1152]{2,1,0:T(8,128)(2,1)S(1)}, u32[]{:S(2)}, u32[]{:S(2)}) async-start(bf16[16,16,1152]{2,1,0:T(8,128)(2,1)} %broadcast_in_dim.20), calls=%async_computation.5 | async-start | bytes 1179648 | tf_op jit(solution)/shard_map/all_to_all | solution.py:47
  216.9 5.8 %shard_map.97.refs_4_ = f32[256,1024]{1,0:T(8,128)S(1)} custom-call(bf16[64,4096]{1,0:T(8,128)(2,1)S(1)} %get-tuple-element.55.refs_0_, bf16[64,4096]{1,0:T(8,128)(2,1)S(1)} %copy-done.7, bf16[64,4096]{1,0:T(8,128)(2,1)S(1)} %copy-done.9, bf16[64,4096]{1,0:T(8,128)(2,1)S(1)} %copy-done.11, bf16[4096,512]{1,0:T(8,128)(2,1)} %shard_map.92.refs_6_.refs_4_, ...), custom_call_target="tpu_custom_call" | custom-call | tf_op jit(solution)/shard_map/pallas_call | solution.py:66
  223.7 5.6 %all-to-all-done.5.refs_1_ = bf16[16,16,1152]{2,1,0:T(8,128)(2,1)S(1)} async-done(((bf16[16,16,1152]{2,1,0:T(8,128)(2,1)}), bf16[16,16,1152]{2,1,0:T(8,128)(2,1)S(1)}, u32[]{:S(2)}, u32[]{:S(2)}) %all-to-all-start.5) | async-done | bytes 589856 | tf_op jit(solution)/shard_map/all_to_all | solution.py:47
  231.6 1.7 shard_map.98
  233.3 13.4 %all_to_all.39.refs_0_ = f32[16,16,128]{2,1,0:T(8,128)S(1)} all-to-all(f32[16,16,128]{2,1,0:T(8,128)S(1)} %shard_map.98), channel_id=1, replica_groups=mesh['zhi'=2,'x'=4,'zlo'=4,'y'=4,'core'=2] {'zlo','y'}, dimensions={0} | all-to-all | bytes 262144 | tf_op jit(solution)/shard_map/all_to_all | solution.py:513
  (119 shorter events, 26.6 us)
Async XLA Ops:
  0.0 45.4 %copy-start.23 = (s32[32]{0:T(128)S(1)}, s32[32]{0:T(128)}, u32[]{:S(2)}) copy-start(s32[32]{0:T(128)} %refs_1_) | copy-start | bytes 388
  0.0 45.4 %copy-start.22 = (s32[32,128]{1,0:T(8,128)S(1)}, s32[32,128]{1,0:T(8,128)}, u32[]{:S(2)}) copy-start(s32[32,128]{1,0:T(8,128)} %refs_3_.1) | copy-start | bytes 49156
  2.0 21.5 %collective-permute-start.2 = (bf16[256,256]{1,0:T(8,128)(2,1)S(1)}, bf16[256,256]{1,0:T(8,128)(2,1)S(1)}, u32[]{:S(2)}, u32[]{:S(2)}) collective-permute-start(bf16[256,256]{1,0:T(8,128)(2,1)S(1)} %pad_maximum_fusion), channel_id=1, source_target_pairs={{0,24},{8,16},{16,8},{24,0},{1,25},{9,17},{17,9},{25,1},{2,26},{10... | collective-permute-start | bytes 393224 | tf_op jit(solution)/shard_map/ppermute | solution.py:27
  6.7 16.8 %collective-permute-start.1 = (bf16[256,256]{1,0:T(8,128)(2,1)S(1)}, bf16[256,256]{1,0:T(8,128)(2,1)S(1)}, u32[]{:S(2)}, u32[]{:S(2)}) collective-permute-start(bf16[256,256]{1,0:T(8,128)(2,1)S(1)} %pad_maximum_fusion), channel_id=1, source_target_pairs={{0,16},{8,24},{16,0},{24,8},{1,17},{9,25},{17,1},{25,9},{2,18},{10... | collective-permute-start | bytes 393224 | tf_op jit(solution)/shard_map/ppermute | solution.py:27
  6.7 16.8 %collective-permute-start = (bf16[256,256]{1,0:T(8,128)(2,1)S(1)}, bf16[256,256]{1,0:T(8,128)(2,1)S(1)}, u32[]{:S(2)}, u32[]{:S(2)}) collective-permute-start(bf16[256,256]{1,0:T(8,128)(2,1)S(1)} %pad_maximum_fusion), channel_id=1, source_target_pairs={{0,8},{8,0},{16,24},{24,16},{1,9},{9,1},{17,25},{25,17},{2,10},{10... | collective-permute-start | bytes 393224 | tf_op jit(solution)/shard_map/ppermute | solution.py:27
  7.4 16.1 %all-to-all-start = ((bf16[16,8,256]{2,1,0:T(8,128)(2,1)}), bf16[16,8,256]{2,1,0:T(8,128)(2,1)S(1)}, u32[]{:S(2)}, u32[]{:S(2)}) async-start(bf16[16,8,256]{2,1,0:T(8,128)(2,1)} %bitcast.26), calls=%async_computation | async-start | bytes 131072 | tf_op jit(solution)/shard_map/all_to_all | solution.py:391
  24.2 9.8 %collective-permute-start.3 = (bf16[2,256,128]{2,1,0:T(8,128)(2,1)S(1)}, bf16[2,256,128]{2,1,0:T(8,128)(2,1)S(1)}, u32[]{:S(2)}, u32[]{:S(2)}) collective-permute-start(bf16[2,256,128]{2,1,0:T(8,128)(2,1)S(1)} %shard_map.84), channel_id=1, source_target_pairs={{0,128},{128,0},{1,129},{129,1},{2,130},{130,2},{3,131},{131,3},{4... | collective-permute-start | bytes 393224 | tf_op jit(solution)/shard_map/ppermute | solution.py:27
  34.0 9.5 %copy-start.18 = (bf16[2,256,128]{2,1,0:T(8,128)(2,1)}, bf16[2,256,128]{2,1,0:T(8,128)(2,1)S(1)}, u32[]{:S(2)}) copy-start(bf16[2,256,128]{2,1,0:T(8,128)(2,1)S(1)} %collective-permute-done.3.refs_2_) | copy-start | bytes 393220
  34.0 19.8 %all-to-all-start.1 = ((bf16[8,8,4096]{2,1,0:T(8,128)(2,1)}), bf16[8,8,4096]{2,1,0:T(8,128)(2,1)S(1)}, u32[]{:S(2)}, u32[]{:S(2)}) async-start(bf16[8,8,4096]{2,1,0:T(8,128)(2,1)} %shard_map.85), calls=%async_computation.1 | async-start | bytes 1048576 | tf_op jit(solution)/shard_map/all_to_all | solution.py:435
  42.3 20.9 %collective-permute-start.7 = (bf16[4,256,256]{2,1,0:T(8,128)(2,1)S(1)}, bf16[4,256,256]{2,1,0:T(8,128)(2,1)}, u32[]{:S(2)}, u32[]{:S(2)}) collective-permute-start(bf16[4,256,256]{2,1,0:T(8,128)(2,1)S(1)} %shard_map.83.refs_1_.refs_4_), channel_id=1, source_target_pairs={{0,4},{2,6},{4,0},{6,2},{1,5},{3,7},{5,1},{7,3},{8,12},{10,14},{12... | collective-permute-start | bytes 1572872 | tf_op jit(solution)/shard_map/ppermute | solution.py:27
  43.5 21.3 %collective-permute-start.6 = (bf16[4,256,256]{2,1,0:T(8,128)(2,1)S(1)}, bf16[4,256,256]{2,1,0:T(8,128)(2,1)}, u32[]{:S(2)}, u32[]{:S(2)}) collective-permute-start(bf16[4,256,256]{2,1,0:T(8,128)(2,1)S(1)} %shard_map.83.refs_1_.refs_4_), channel_id=1, source_target_pairs={{0,6},{2,4},{4,2},{6,0},{1,7},{3,5},{5,3},{7,1},{8,14},{10,12},{12... | collective-permute-start | bytes 1572872 | tf_op jit(solution)/shard_map/ppermute | solution.py:27
  51.5 17.5 %collective-permute-start.4 = (bf16[128,4096]{1,0:T(8,128)(2,1)}, bf16[128,4096]{1,0:T(8,128)(2,1)}, u32[]{:S(2)}, u32[]{:S(2)}) collective-permute-start(bf16[128,4096]{1,0:T(8,128)(2,1)} %get-tuple-element.45), channel_id=1, source_target_pairs={{0,1},{1,0},{2,3},{3,2},{4,5},{5,4},{6,7},{7,6},{8,9},{9,8},{10,11... | collective-permute-start | bytes 3145736 | tf_op jit(solution)/shard_map/ppermute | solution.py:27
  52.1 18.4 %copy-start.3 = (bf16[128,4096]{1,0:T(8,128)(2,1)S(1)}, bf16[128,4096]{1,0:T(8,128)(2,1)}, u32[]{:S(2)}) copy-start(bf16[128,4096]{1,0:T(8,128)(2,1)} %copy-done.2) | copy-start | bytes 3145732
  52.1 14.7 %collective-permute-start.5 = (bf16[4,256,256]{2,1,0:T(8,128)(2,1)S(1)}, bf16[4,256,256]{2,1,0:T(8,128)(2,1)}, u32[]{:S(2)}, u32[]{:S(2)}) collective-permute-start(bf16[4,256,256]{2,1,0:T(8,128)(2,1)S(1)} %shard_map.83.refs_1_.refs_4_), channel_id=1, source_target_pairs={{0,2},{2,0},{4,6},{6,4},{1,3},{3,1},{5,7},{7,5},{8,10},{10,8},{12,... | collective-permute-start | bytes 1572872 | tf_op jit(solution)/shard_map/ppermute | solution.py:27
  52.6 8.5 %collective-permute-start.12 = (bf16[32,4096]{1,0:T(8,128)(2,1)S(1)}, bf16[32,4096]{1,0:T(8,128)(2,1)}, u32[]{:S(2)}, u32[]{:S(2)}) collective-permute-start(bf16[32,4096]{1,0:T(8,128)(2,1)S(1)} %shard_map.88.refs_0_), channel_id=1, source_target_pairs={{0,8},{8,0},{16,24},{24,16},{1,9},{9,1},{17,25},{25,17},{2,10},{10... | collective-permute-start | bytes 786440 | tf_op jit(solution)/shard_map/ppermute | solution.py:27
  61.1 37.5 %collective-permute-start.22 = (bf16[1024,512]{1,0:T(8,128)(2,1)S(1)}, bf16[1024,512]{1,0:T(8,128)(2,1)S(1)}, u32[]{:S(2)}, u32[]{:S(2)}) collective-permute-start(bf16[1024,512]{1,0:T(8,128)(2,1)S(1)} %multiply_convert_fusion.refs_0_), channel_id=1, source_target_pairs={{0,64},{32,96},{64,0},{96,32},{1,65},{33,97},{65,1},{97,33},{2,66}... | collective-permute-start | bytes 3145736 | tf_op jit(solution)/shard_map/ppermute | solution.py:27
  63.2 46.4 %collective-permute-start.21 = (bf16[1024,512]{1,0:T(8,128)(2,1)S(1)}, bf16[1024,512]{1,0:T(8,128)(2,1)S(1)}, u32[]{:S(2)}, u32[]{:S(2)}) collective-permute-start(bf16[1024,512]{1,0:T(8,128)(2,1)S(1)} %multiply_convert_fusion.refs_0_), channel_id=1, source_target_pairs={{0,96},{32,64},{64,32},{96,0},{1,97},{33,65},{65,33},{97,1},{2,98}... | collective-permute-start | bytes 3145736 | tf_op jit(solution)/shard_map/ppermute | solution.py:27
  64.8 44.9 %collective-permute-start.20 = (bf16[1024,512]{1,0:T(8,128)(2,1)S(1)}, bf16[1024,512]{1,0:T(8,128)(2,1)S(1)}, u32[]{:S(2)}, u32[]{:S(2)}) collective-permute-start(bf16[1024,512]{1,0:T(8,128)(2,1)S(1)} %multiply_convert_fusion.refs_0_), channel_id=1, source_target_pairs={{0,32},{32,0},{64,96},{96,64},{1,33},{33,1},{65,97},{97,65},{2,34}... | collective-permute-start | bytes 3145736 | tf_op jit(solution)/shard_map/ppermute | solution.py:27
  66.8 25.5 %collective-permute-start.13 = (bf16[64,4096]{1,0:T(8,128)(2,1)S(1)}, bf16[64,4096]{1,0:T(8,128)(2,1)S(1)}, u32[]{:S(2)}, u32[]{:S(2)}) collective-permute-start(bf16[64,4096]{1,0:T(8,128)(2,1)S(1)} %shard_map.89.refs_0_), channel_id=1, source_target_pairs={{0,16},{8,24},{16,0},{24,8},{1,17},{9,25},{17,1},{25,9},{2,18},{10... | collective-permute-start | bytes 1572872 | tf_op jit(solution)/shard_map/ppermute | solution.py:27
  69.0 6.7 %collective-permute-start.11 = (bf16[2,256,128]{2,1,0:T(8,128)(2,1)}, bf16[2,256,128]{2,1,0:T(8,128)(2,1)S(1)}, u32[]{:S(2)}, u32[]{:S(2)}) collective-permute-start(bf16[2,256,128]{2,1,0:T(8,128)(2,1)} %copy-done.18), channel_id=1, source_target_pairs={{0,4},{2,6},{4,0},{6,2},{1,5},{3,7},{5,1},{7,3},{8,12},{10,14},{12... | collective-permute-start | bytes 393224 | tf_op jit(solution)/shard_map/ppermute | solution.py:27
  70.5 21.9 %copy-start.19 = (bf16[2,256,128]{2,1,0:T(8,128)(2,1)S(1)}, bf16[2,256,128]{2,1,0:T(8,128)(2,1)}, u32[]{:S(2)}) copy-start(bf16[2,256,128]{2,1,0:T(8,128)(2,1)} %copy-done.18) | copy-start | bytes 393220
  73.1 36.5 %copy-start.12 = (bf16[8,256,128]{2,1,0:T(8,128)(2,1)}, bf16[8,256,128]{2,1,0:T(8,128)(2,1)S(1)}, u32[]{:S(2)}) copy-start(bf16[8,256,128]{2,1,0:T(8,128)(2,1)S(1)} %get-tuple-element.59.refs_1_) | copy-start | bytes 1572868
  75.7 18.0 %collective-permute-start.8 = (f32[288,128]{1,0:T(8,128)S(1)}, f32[288,128]{1,0:T(8,128)S(1)}, u32[]{:S(2)}, u32[]{:S(2)}) collective-permute-start(f32[288,128]{1,0:T(8,128)S(1)} %get-tuple-element.48), channel_id=1, source_target_pairs={{0,1},{1,0},{2,3},{3,2},{4,5},{5,4},{6,7},{7,6},{8,9},{9,8},{10,11... | collective-permute-start | bytes 442376 | tf_op jit(solution)/shard_map/ppermute | solution.py:27
  92.3 6.2 %collective-permute-start.10 = (bf16[2,256,128]{2,1,0:T(8,128)(2,1)S(1)}, bf16[2,256,128]{2,1,0:T(8,128)(2,1)S(1)}, u32[]{:S(2)}, u32[]{:S(2)}) collective-permute-start(bf16[2,256,128]{2,1,0:T(8,128)(2,1)S(1)} %copy-done.19), channel_id=1, source_target_pairs={{0,6},{2,4},{4,2},{6,0},{1,7},{3,5},{5,3},{7,1},{8,14},{10,12},{12... | collective-permute-start | bytes 393224 | tf_op jit(solution)/shard_map/ppermute | solution.py:27
  93.7 5.0 %collective-permute-start.9 = (bf16[2,256,128]{2,1,0:T(8,128)(2,1)S(1)}, bf16[2,256,128]{2,1,0:T(8,128)(2,1)S(1)}, u32[]{:S(2)}, u32[]{:S(2)}) collective-permute-start(bf16[2,256,128]{2,1,0:T(8,128)(2,1)S(1)} %copy-done.19), channel_id=1, source_target_pairs={{0,2},{2,0},{4,6},{6,4},{1,3},{3,1},{5,7},{7,5},{8,10},{10,8},{12,... | collective-permute-start | bytes 393224 | tf_op jit(solution)/shard_map/ppermute | solution.py:27
  109.6 34.9 %copy-start.13 = (bf16[8,256,128]{2,1,0:T(8,128)(2,1)S(1)}, bf16[8,256,128]{2,1,0:T(8,128)(2,1)}, u32[]{:S(2)}) copy-start(bf16[8,256,128]{2,1,0:T(8,128)(2,1)} %copy-done.12) | copy-start | bytes 1572868
  111.9 32.6 %collective-permute-start.23 = (bf16[4096,512]{1,0:T(8,128)(2,1)}, bf16[4096,512]{1,0:T(8,128)(2,1)}, u32[]{:S(2)}, u32[]{:S(2)}) collective-permute-start(bf16[4096,512]{1,0:T(8,128)(2,1)} %shard_map.92.refs_6_.refs_4_), channel_id=1, source_target_pairs={{0,1},{1,0},{2,3},{3,2},{4,5},{5,4},{6,7},{7,6},{8,9},{9,8},{10,11... | collective-permute-start | bytes 12582920 | tf_op jit(solution)/shard_map/ppermute | solution.py:27
  111.9 16.2 %collective-permute-start.15 = (bf16[64,4096]{1,0:T(8,128)(2,1)}, bf16[64,4096]{1,0:T(8,128)(2,1)}, u32[]{:S(2)}, u32[]{:S(2)}) collective-permute-start(bf16[64,4096]{1,0:T(8,128)(2,1)} %get-tuple-element.54.refs_0_), channel_id=1, source_target_pairs={{0,6},{2,4},{4,2},{6,0},{1,7},{3,5},{5,3},{7,1},{8,14},{10,12},{12... | collective-permute-start | bytes 1572872 | tf_op jit(solution)/shard_map/ppermute | solution.py:27
  113.5 15.0 %collective-permute-start.16 = (bf16[64,4096]{1,0:T(8,128)(2,1)S(1)}, bf16[64,4096]{1,0:T(8,128)(2,1)S(1)}, u32[]{:S(2)}, u32[]{:S(2)}) collective-permute-start(bf16[64,4096]{1,0:T(8,128)(2,1)S(1)} %get-tuple-element.55.refs_0_), channel_id=1, source_target_pairs={{0,2},{2,0},{4,6},{6,4},{1,3},{3,1},{5,7},{7,5},{8,10},{10,8},{12,... | collective-permute-start | bytes 1572872 | tf_op jit(solution)/shard_map/ppermute | solution.py:27
  114.3 25.4 %collective-permute-start.14 = (bf16[64,4096]{1,0:T(8,128)(2,1)}, bf16[64,4096]{1,0:T(8,128)(2,1)}, u32[]{:S(2)}, u32[]{:S(2)}) collective-permute-start(bf16[64,4096]{1,0:T(8,128)(2,1)} %get-tuple-element.54.refs_0_), channel_id=1, source_target_pairs={{0,2},{2,0},{4,6},{6,4},{1,3},{3,1},{5,7},{7,5},{8,10},{10,8},{12,... | collective-permute-start | bytes 1572872 | tf_op jit(solution)/shard_map/ppermute | solution.py:27
  115.6 24.1 %collective-permute-start.17 = (bf16[64,4096]{1,0:T(8,128)(2,1)S(1)}, bf16[64,4096]{1,0:T(8,128)(2,1)S(1)}, u32[]{:S(2)}, u32[]{:S(2)}) collective-permute-start(bf16[64,4096]{1,0:T(8,128)(2,1)S(1)} %get-tuple-element.55.refs_0_), channel_id=1, source_target_pairs={{0,6},{2,4},{4,2},{6,0},{1,7},{3,5},{5,3},{7,1},{8,14},{10,12},{12... | collective-permute-start | bytes 1572872 | tf_op jit(solution)/shard_map/ppermute | solution.py:27
  117.2 19.1 %all-to-all-start.2 = ((f32[8,64,128]{2,1,0:T(8,128)}), f32[8,64,128]{2,1,0:T(8,128)S(1)}, u32[]{:S(2)}, u32[]{:S(2)}) async-start(f32[8,64,128]{2,1,0:T(8,128)} %shard_map.87), calls=%async_computation.2 | async-start | bytes 524288 | tf_op jit(solution)/shard_map/all_to_all | solution.py:456
  128.1 24.8 %collective-permute-start.18 = (bf16[64,4096]{1,0:T(8,128)(2,1)}, bf16[64,4096]{1,0:T(8,128)(2,1)}, u32[]{:S(2)}, u32[]{:S(2)}) collective-permute-start(bf16[64,4096]{1,0:T(8,128)(2,1)} %collective-permute-done.15.refs_2_), channel_id=1, source_target_pairs={{0,2},{2,0},{4,6},{6,4},{1,3},{3,1},{5,7},{7,5},{8,10},{10,8},{12,... | collective-permute-start | bytes 1572872 | tf_op jit(solution)/shard_map/ppermute | solution.py:27
  128.6 21.4 %copy-start.6 = (bf16[64,4096]{1,0:T(8,128)(2,1)}, bf16[64,4096]{1,0:T(8,128)(2,1)S(1)}, u32[]{:S(2)}) copy-start(bf16[64,4096]{1,0:T(8,128)(2,1)S(1)} %collective-permute-done.16.refs_1_) | copy-start | bytes 1572868
  128.6 24.3 %collective-permute-start.19 = (bf16[64,4096]{1,0:T(8,128)(2,1)S(1)}, bf16[64,4096]{1,0:T(8,128)(2,1)S(1)}, u32[]{:S(2)}, u32[]{:S(2)}) collective-permute-start(bf16[64,4096]{1,0:T(8,128)(2,1)S(1)} %collective-permute-done.16.refs_1_), channel_id=1, source_target_pairs={{0,6},{2,4},{4,2},{6,0},{1,7},{3,5},{5,3},{7,1},{8,14},{10,12},{12... | collective-permute-start | bytes 1572872 | tf_op jit(solution)/shard_map/ppermute | solution.py:27
  140.4 12.5 %all-to-all-start.3 = ((bf16[4,32,1024]{2,1,0:T(8,128)(2,1)}), bf16[4,32,1024]{2,1,0:T(8,128)(2,1)}, u32[]{:S(2)}, u32[]{:S(2)}) async-start(bf16[4,32,1024]{2,1,0:T(8,128)(2,1)} %broadcast_in_dim.18), calls=%async_computation.3 | async-start | bytes 524288 | tf_op jit(solution)/shard_map/all_to_all | solution.py:47
  150.0 9.4 %collective-permute-start.24 = (bf16[128,1024]{1,0:T(8,128)(2,1)}, bf16[128,1024]{1,0:T(8,128)(2,1)S(1)}, u32[]{:S(2)}, u32[]{:S(2)}) collective-permute-start(bf16[128,1024]{1,0:T(8,128)(2,1)} %get-tuple-element.66), channel_id=1, source_target_pairs={{0,1},{1,0},{2,3},{3,2},{4,5},{5,4},{6,7},{7,6},{8,9},{9,8},{10,11... | collective-permute-start | bytes 786440 | tf_op jit(solution)/shard_map/ppermute | solution.py:27
  152.9 6.5 %copy-start.10 = (bf16[64,4096]{1,0:T(8,128)(2,1)}, bf16[64,4096]{1,0:T(8,128)(2,1)S(1)}, u32[]{:S(2)}) copy-start(bf16[64,4096]{1,0:T(8,128)(2,1)S(1)} %collective-permute-done.19.refs_3_) | copy-start | bytes 1572868
  155.1 17.5 %all-to-all-start.4 = ((bf16[4,4,32,1024]{3,2,1,0:T(8,128)(2,1)}), bf16[4,4,32,1024]{3,2,1,0:T(8,128)(2,1)}, u32[]{:S(2)}, u32[]{:S(2)}) async-start(bf16[4,4,32,1024]{3,2,1,0:T(8,128)(2,1)} %broadcast_in_dim.19), calls=%async_computation.4 | async-start | bytes 2097152 | tf_op jit(solution)/shard_map/all_to_all | solution.py:47
  159.5 12.0 %collective-permute-start.25 = (bf16[128,1024]{1,0:T(8,128)(2,1)S(1)}, bf16[128,1024]{1,0:T(8,128)(2,1)S(1)}, u32[]{:S(2)}, u32[]{:S(2)}) collective-permute-start(bf16[128,1024]{1,0:T(8,128)(2,1)S(1)} %fusion.1), channel_id=1, source_target_pairs={{0,128},{128,0},{1,129},{129,1},{2,130},{130,2},{3,131},{131,3},{4... | collective-permute-start | bytes 786440 | tf_op jit(solution)/shard_map/ppermute | solution.py:27
  174.6 10.3 %collective-permute-start.26 = (bf16[512,1024]{1,0:T(8,128)(2,1)S(1)}, bf16[512,1024]{1,0:T(8,128)(2,1)S(1)}, u32[]{:S(2)}, u32[]{:S(2)}) collective-permute-start(bf16[512,1024]{1,0:T(8,128)(2,1)S(1)} %convolution_convert_fusion.refs_2_), channel_id=1, source_target_pairs={{0,1},{1,0},{2,3},{3,2},{4,5},{5,4},{6,7},{7,6},{8,9},{9,8},{10,11... | collective-permute-start | bytes 3145736 | tf_op jit(solution)/shard_map/ppermute | solution.py:27
  174.7 18.4 %collective-permute-start.27 = (bf16[256,1024]{1,0:T(8,128)(2,1)S(1)}, bf16[256,1024]{1,0:T(8,128)(2,1)S(1)}, u32[]{:S(2)}, u32[]{:S(2)}) collective-permute-start(bf16[256,1024]{1,0:T(8,128)(2,1)S(1)} %shard_map.94), channel_id=1, source_target_pairs={{0,128},{128,0},{1,129},{129,1},{2,130},{130,2},{3,131},{131,3},{4... | collective-permute-start | bytes 1572872 | tf_op jit(solution)/shard_map/ppermute | solution.py:27
  180.1 12.9 %collective-permute-start.30 = (bf16[128,1024]{1,0:T(8,128)(2,1)S(1)}, bf16[128,1024]{1,0:T(8,128)(2,1)S(1)}, u32[]{:S(2)}, u32[]{:S(2)}) collective-permute-start(bf16[128,1024]{1,0:T(8,128)(2,1)S(1)} %add_convert_fusion.refs_0_), channel_id=1, source_target_pairs={{0,64},{32,96},{64,0},{96,32},{1,65},{33,97},{65,1},{97,33},{2,66}... | collective-permute-start | bytes 786440 | tf_op jit(solution)/shard_map/ppermute | solution.py:27
  182.2 13.4 %collective-permute-start.29 = (bf16[128,1024]{1,0:T(8,128)(2,1)S(1)}, bf16[128,1024]{1,0:T(8,128)(2,1)S(1)}, u32[]{:S(2)}, u32[]{:S(2)}) collective-permute-start(bf16[128,1024]{1,0:T(8,128)(2,1)S(1)} %add_convert_fusion.refs_0_), channel_id=1, source_target_pairs={{0,96},{32,64},{64,32},{96,0},{1,97},{33,65},{65,33},{97,1},{2,98}... | collective-permute-start | bytes 786440 | tf_op jit(solution)/shard_map/ppermute | solution.py:27
  182.2 13.4 %collective-permute-start.28 = (bf16[128,1024]{1,0:T(8,128)(2,1)S(1)}, bf16[128,1024]{1,0:T(8,128)(2,1)S(1)}, u32[]{:S(2)}, u32[]{:S(2)}) collective-permute-start(bf16[128,1024]{1,0:T(8,128)(2,1)S(1)} %add_convert_fusion.refs_0_), channel_id=1, source_target_pairs={{0,32},{32,0},{64,96},{96,64},{1,33},{33,1},{65,97},{97,65},{2,34}... | collective-permute-start | bytes 786440 | tf_op jit(solution)/shard_map/ppermute | solution.py:27
  196.5 32.8 %all-to-all-start.5 = ((bf16[16,16,1152]{2,1,0:T(8,128)(2,1)}), bf16[16,16,1152]{2,1,0:T(8,128)(2,1)S(1)}, u32[]{:S(2)}, u32[]{:S(2)}) async-start(bf16[16,16,1152]{2,1,0:T(8,128)(2,1)} %broadcast_in_dim.20), calls=%async_computation.5 | async-start | bytes 1179648 | tf_op jit(solution)/shard_map/all_to_all | solution.py:47
  213.6 9.0 %collective-permute-start.31 = (bf16[512,1024]{1,0:T(8,128)(2,1)S(1)}, bf16[512,1024]{1,0:T(8,128)(2,1)S(1)}, u32[]{:S(2)}, u32[]{:S(2)}) collective-permute-start(bf16[512,1024]{1,0:T(8,128)(2,1)S(1)} %shard_map.96.refs_2_), channel_id=1, source_target_pairs={{0,1},{1,0},{2,3},{3,2},{4,5},{5,4},{6,7},{7,6},{8,9},{9,8},{10,11... | collective-permute-start | bytes 3145736 | tf_op jit(solution)/shard_map/ppermute | solution.py:27
  216.9 12.5 %copy-start.21 = (s32[256,1]{1,0:T(8,128)S(1)}, s32[256,1]{1,0:T(8,128)}, u32[]{:S(2)}) copy-start(s32[256,1]{1,0:T(8,128)} %copy-done.20) | copy-start | bytes 3076
  (16 other events, 24.8 us)

commit v2 on v1

--- a/solution.py
+++ b/solution.py
@@ -406,7 +406,7 @@
             ((plane * rows, 1), jnp.int32, "v"),
             ((micro,), jnp.int32, "s"),
         ],
-        [where, tied(exit_section, came)],
+        [where, exit_section],
         [inputs, targets],
         scratch=[pltpu.SMEM((sections,), jnp.int32)],
     )
@@ -417,6 +417,7 @@
         leaving_kernel, [((2, features, rank), BF16, "v")], [where], [lined]
     )
     up_came = hop(leaving, "zhi", 1)
+    head_pieces = direct(tied(scaled_head, up_came), "x", RING)
     partner_rows = hop(tied(other_rows, up_came), "core", 1)
 
     (state,) = kernel_call(
@@ -429,7 +430,7 @@
     state = [state, hop(state, "zlo", 2)]
 
     (copies,) = kernel_call(
-        up_kernel, [((sections, own_rank, width // 2), BF16, "v")], [where], [came]
+        up_kernel, [((sections, own_rank, width // 2), BF16, "v")], [where], [tied(came, own_square)]
     )
     copies = tied(copies, up_came)
     up_rows = lax.all_to_all(copies, SECTION, 0, 0, tiled=True)
@@ -447,7 +448,6 @@
     (outgoing,) = kernel_call(
         combine_kernel, [((sections, 4 * rows, rank), F32, "v")], [], [keep, hop(send, "core", 1)]
     )
-    head_pieces = direct(tied(scaled_head, up_rows), "x", RING)
     line_rows = ((4 * rows, width // 2), BF16, "v")
     state = kernel_call(part_kernel, [line_rows, line_rows], [], [tied(part, send) for part in state])
     passing, staying = ring(*state, "y")

time: 249 us -> 244 us (0.980)
  starting transfers between devices: 95.2 us -> 86.6 us
  local copies, waits for them, and re-layouts: 16.3 us -> 20.8 us
  waiting for transfers between devices: 83.1 us -> 79.2 us
    ppermute x32, starting transfers between devices: 45.5 us -> 39.1 us  [hop(): return lax.ppermute(block, axis, [(i, i ^ bit) for i in range(size)])]
    unnamed x51 -> x53, local copies, waits for them, and re-layouts: 11.6 us -> 15.3 us
    ppermute x32, waiting for transfers between devices: 59 us -> 55.5 us  [hop(): return lax.ppermute(block, axis, [(i, i ^ bit) for i in range(size)])]
    all_to_all x1, starting transfers between devices: 8.27 us -> 5.71 us  [per_device(): up_rows = lax.all_to_all(copies, SECTION, 0, 0, tiled=True)]
  transfers between devices with their start and end apart: 38 -> 38, of which waited for: 17 -> 16; matrix products, arithmetic and copies ran while one was open for 2% -> 2% of each run, Pallas kernels for 12% -> 13%
where the time goes in v2:
time: 244 us; the launch traced here: 243 us
  starting transfers between devices  86.6 us (35%)
  waiting for transfers between devices  79.2 us (32%)
  Pallas kernels  37.3 us (15%)
  local copies, waits for them, and re-layouts  20.8 us (9%)
  blocking collectives  13.4 us (5%)
  other arithmetic  2.9 us (1%)
    ppermute x32, waiting for transfers between devices, hop(): return lax.ppermute(block, axis, [(i, i ^ bit) for i in range(size)])  55.5 us
    ppermute x32, starting transfers between devices, hop(): return lax.ppermute(block, axis, [(i, i ^ bit) for i in range(size)])  39.1 us
    pallas_call x18, Pallas kernels, kernel_call(): pl.pallas_call(inner, out_shape=shapes, in_specs=[small] * len(scalars) +...  37.3 us
    all_to_all x3, starting transfers between devices, spread(): return lax.all_to_all(copies, axis, 0, 0, tiled=True)  26.9 us
    unnamed x53, local copies, waits for them, and re-layouts  15.3 us
    all_to_all x1, blocking collectives, per_device(): sums = lax.all_to_all(sums, PLANE, 0, 0, tiled=True)  13.4 us
    all_to_all x3, waiting for transfers between devices, spread(): return lax.all_to_all(copies, axis, 0, 0, tiled=True)  11.1 us
    all_to_all x1, waiting for transfers between devices, per_device(): lax.all_to_all(up, PLANE, 0, 0, tiled=True)  8.31 us
  transfers between devices with their start and end apart: 38, of which 16 were waited for; matrix products, arithmetic and copies ran while one was open for 2% of the time, Pallas kernels for 13%

profile of v2, /device:TPU:2, one launch (start us, length us, event | category | flops | bytes accessed | tf_op | source)
XLA Modules:
  0.0 242.6 jit_solution(11826536370783204424)
XLA Ops:
  2.0 4.7 %collective-permute-start.2 = (bf16[256,256]{1,0:T(8,128)(2,1)S(1)}, bf16[256,256]{1,0:T(8,128)(2,1)S(1)}, u32[]{:S(2)}, u32[]{:S(2)}) collective-permute-start(bf16[256,256]{1,0:T(8,128)(2,1)S(1)} %pad_maximum_fusion), channel_id=1, source_target_pairs={{0,24},{8,16},{16,8},{24,0},{1,25},{9,17},{17,9},{25,1},{2,26},{10... | collective-permute-start | bytes 393224 | tf_op jit(solution)/shard_map/ppermute | solution.py:27
  7.4 7.7 %all-to-all-start = ((bf16[16,8,256]{2,1,0:T(8,128)(2,1)}), bf16[16,8,256]{2,1,0:T(8,128)(2,1)S(1)}, u32[]{:S(2)}, u32[]{:S(2)}) async-start(bf16[16,8,256]{2,1,0:T(8,128)(2,1)} %bitcast.26), calls=%async_computation | async-start | bytes 131072 | tf_op jit(solution)/shard_map/all_to_all | solution.py:391
  15.2 8.3 %all-to-all-done.refs_1_ = bf16[16,8,256]{2,1,0:T(8,128)(2,1)S(1)} async-done(((bf16[16,8,256]{2,1,0:T(8,128)(2,1)}), bf16[16,8,256]{2,1,0:T(8,128)(2,1)S(1)}, u32[]{:S(2)}, u32[]{:S(2)}) %all-to-all-start) | async-done | bytes 65568 | tf_op jit(solution)/shard_map/all_to_all | solution.py:391
  24.2 4.6 %collective-permute-start.3 = (bf16[2,256,128]{2,1,0:T(8,128)(2,1)S(1)}, bf16[2,256,128]{2,1,0:T(8,128)(2,1)}, u32[]{:S(2)}, u32[]{:S(2)}) collective-permute-start(bf16[2,256,128]{2,1,0:T(8,128)(2,1)S(1)} %shard_map.84), channel_id=1, source_target_pairs={{0,128},{128,0},{1,129},{129,1},{2,130},{130,2},{3,131},{131,3},{4... | collective-permute-start | bytes 393224 | tf_op jit(solution)/shard_map/ppermute | solution.py:27
  29.7 2.3 collective-permute-start.6
  32.0 1.6 copy-done.1
  33.6 2.9 %shard_map.82 = (bf16[128,4096]{1,0:T(8,128)(2,1)S(1)}, bf16[128,4096]{1,0:T(8,128)(2,1)}, f32[16,1]{1,0:T(8,128)S(1)}, bf16[128,8192]{1,0:T(8,128)(2,1)S(1)}, s32[256,1]{1,0:T(8,128)S(1)}, /*index=5*/s32[32]{0:T(128)}) custom-call(s32[7]{0:T(128)S(1)} %stack.27.refs_0_, s32[32]{0:T(128)S(1)} %copy-done.25, bf16[32,4,8192]{2,1,0:T(4,128)(2,1)S(1)} %copy-done.1, ...), custom_call_target="tpu_custom_call" | custom-call | tf_op jit(solution)/shard_map/pallas_call | solution.py:66
  39.4 1.4 shard_map.85
  41.3 5.7 %all-to-all-start.1 = ((bf16[8,8,4096]{2,1,0:T(8,128)(2,1)}), bf16[8,8,4096]{2,1,0:T(8,128)(2,1)S(1)}, u32[]{:S(2)}, u32[]{:S(2)}) async-start(bf16[8,8,4096]{2,1,0:T(8,128)(2,1)} %shard_map.85), calls=%async_computation.1 | async-start | bytes 1048576 | tf_op jit(solution)/shard_map/all_to_all | solution.py:436
  47.0 1.5 multiply_convert_fusion.refs_0_
  48.5 7.0 %collective-permute-done.12.refs_1_ = bf16[32,4096]{1,0:T(8,128)(2,1)S(1)} collective-permute-done((bf16[32,4096]{1,0:T(8,128)(2,1)S(1)}, bf16[32,4096]{1,0:T(8,128)(2,1)S(1)}, u32[]{:S(2)}, u32[]{:S(2)}) %collective-permute-start.12) | collective-permute-done | bytes 262176 | tf_op jit(solution)/shard_map/ppermute | solution.py:27
  56.2 2.2 collective-permute-start.22
  58.4 2.5 %collective-permute-start.20 = (bf16[1024,512]{1,0:T(8,128)(2,1)S(1)}, bf16[1024,512]{1,0:T(8,128)(2,1)}, u32[]{:S(2)}, u32[]{:S(2)}) collective-permute-start(bf16[1024,512]{1,0:T(8,128)(2,1)S(1)} %multiply_convert_fusion.refs_0_), channel_id=1, source_target_pairs={{0,32},{32,0},{64,96},{96,64},{1,33},{33,1},{65,97},{97,65},{2,34}... | collective-permute-start | bytes 3145736 | tf_op jit(solution)/shard_map/ppermute | solution.py:27
  62.2 1.2 copy-done.3
  63.4 2.4 shard_map.86
  65.8 3.0 %collective-permute-done.11.refs_5_ = bf16[2,256,128]{2,1,0:T(8,128)(2,1)S(1)} collective-permute-done((bf16[2,256,128]{2,1,0:T(8,128)(2,1)}, bf16[2,256,128]{2,1,0:T(8,128)(2,1)S(1)}, u32[]{:S(2)}, u32[]{:S(2)}) %collective-permute-start.11) | collective-permute-done | bytes 131104 | tf_op jit(solution)/shard_map/ppermute | solution.py:27
  69.5 16.9 %collective-permute-done.13.refs_1_ = bf16[64,4096]{1,0:T(8,128)(2,1)} collective-permute-done((bf16[64,4096]{1,0:T(8,128)(2,1)S(1)}, bf16[64,4096]{1,0:T(8,128)(2,1)}, u32[]{:S(2)}, u32[]{:S(2)}) %collective-permute-start.13) | collective-permute-done | bytes 524320 | tf_op jit(solution)/shard_map/ppermute | solution.py:27
  88.1 1.9 shard_map.90
  90.7 2.4 %collective-permute-done.10.refs_4_ = bf16[2,256,128]{2,1,0:T(8,128)(2,1)S(1)} collective-permute-done((bf16[2,256,128]{2,1,0:T(8,128)(2,1)}, bf16[2,256,128]{2,1,0:T(8,128)(2,1)S(1)}, u32[]{:S(2)}, u32[]{:S(2)}) %collective-permute-start.10) | collective-permute-done | bytes 131104 | tf_op jit(solution)/shard_map/ppermute | solution.py:27
  93.2 8.5 %collective-permute-done.21.refs_2_ = bf16[1024,512]{1,0:T(8,128)(2,1)} collective-permute-done((bf16[1024,512]{1,0:T(8,128)(2,1)S(1)}, bf16[1024,512]{1,0:T(8,128)(2,1)}, u32[]{:S(2)}, u32[]{:S(2)}) %collective-permute-start.21) | collective-permute-done | bytes 1048608 | tf_op jit(solution)/shard_map/ppermute | solution.py:27
  101.9 4.2 %shard_map.92.refs_6_.refs_4_ = bf16[4096,512]{1,0:T(8,128)(2,1)} custom-call(bf16[1024,512]{1,0:T(8,128)(2,1)S(1)} %multiply_convert_fusion.refs_0_, bf16[1024,512]{1,0:T(8,128)(2,1)} %collective-permute-done.20.refs_1_, bf16[1024,512]{1,0:T(8,128)(2,1)} %collective-permute-done.21.refs_2_, bf16[1024,512]{1,0:T(8,128)(2,1)} %collective-permute-done.22.refs_3_), custom_call_target="tpu_custom_call" | custom-call | tf_op jit(solution)/shard_map/pallas_call | solution.py:66
  106.0 1.2 collective-permute-start.15
  109.3 2.0 collective-permute-start.17
  111.3 7.2 %all-to-all-start.2 = ((f32[8,64,128]{2,1,0:T(8,128)}), f32[8,64,128]{2,1,0:T(8,128)S(1)}, u32[]{:S(2)}, u32[]{:S(2)}) async-start(f32[8,64,128]{2,1,0:T(8,128)} %shard_map.87), calls=%async_computation.2 | async-start | bytes 524288 | tf_op jit(solution)/shard_map/all_to_all | solution.py:456
  118.5 3.8 %collective-permute-done.15.refs_2_ = bf16[64,4096]{1,0:T(8,128)(2,1)} collective-permute-done((bf16[64,4096]{1,0:T(8,128)(2,1)}, bf16[64,4096]{1,0:T(8,128)(2,1)}, u32[]{:S(2)}, u32[]{:S(2)}) %collective-permute-start.15) | collective-permute-done | bytes 524320 | tf_op jit(solution)/shard_map/ppermute | solution.py:27
  124.0 4.3 %all-to-all-done.2.refs_0_.refs_1_ = f32[8,64,128]{2,1,0:T(8,128)S(1)} async-done(((f32[8,64,128]{2,1,0:T(8,128)}), f32[8,64,128]{2,1,0:T(8,128)S(1)}, u32[]{:S(2)}, u32[]{:S(2)}) %all-to-all-start.2) | async-done | bytes 262176 | tf_op jit(solution)/shard_map/all_to_all | solution.py:456
  128.3 5.0 %collective-permute-done.14.refs_1_ = bf16[64,4096]{1,0:T(8,128)(2,1)} collective-permute-done((bf16[64,4096]{1,0:T(8,128)(2,1)}, bf16[64,4096]{1,0:T(8,128)(2,1)}, u32[]{:S(2)}, u32[]{:S(2)}) %collective-permute-start.14) | collective-permute-done | bytes 524320 | tf_op jit(solution)/shard_map/ppermute | solution.py:27
  134.2 4.0 %all-to-all-start.3 = ((bf16[4,32,1024]{2,1,0:T(8,128)(2,1)}), bf16[4,32,1024]{2,1,0:T(8,128)(2,1)}, u32[]{:S(2)}, u32[]{:S(2)}) async-start(bf16[4,32,1024]{2,1,0:T(8,128)(2,1)} %broadcast_in_dim.18), calls=%async_computation.3 | async-start | bytes 524288 | tf_op jit(solution)/shard_map/all_to_all | solution.py:47
  138.3 5.5 %shard_map.93 = (f32[128,1024]{1,0:T(8,128)S(1)}, bf16[128,1024]{1,0:T(8,128)(2,1)}) custom-call(s32[7]{0:T(128)S(1)} %stack.27.refs_0_, bf16[8,256,128]{2,1,0:T(8,128)(2,1)S(1)} %copy-done.13, bf16[2,256,128]{2,1,0:T(8,128)(2,1)} %collective-permute-done.3.refs_2_, bf16[2,256,128]{2,1,0:T(8,128)(2,1)S(1)} %collective-permute-done.9.refs_3_, ...), custom_call_target="tpu_custom_call" | custom-call | tf_op jit(solution)/shard_map/pallas_call | solution.py:66
  143.8 3.2 %all-to-all-done.3 = bf16[4,32,1024]{2,1,0:T(8,128)(2,1)} async-done(((bf16[4,32,1024]{2,1,0:T(8,128)(2,1)}), bf16[4,32,1024]{2,1,0:T(8,128)(2,1)}, u32[]{:S(2)}, u32[]{:S(2)}) %all-to-all-start.3) | async-done | bytes 262176 | tf_op jit(solution)/shard_map/all_to_all | solution.py:47
  147.0 2.2 broadcast_in_dim.19
  149.2 4.2 %all-to-all-start.4 = ((bf16[4,4,32,1024]{3,2,1,0:T(8,128)(2,1)}), bf16[4,4,32,1024]{3,2,1,0:T(8,128)(2,1)}, u32[]{:S(2)}, u32[]{:S(2)}) async-start(bf16[4,4,32,1024]{3,2,1,0:T(8,128)(2,1)} %broadcast_in_dim.19), calls=%async_computation.4 | async-start | bytes 2097152 | tf_op jit(solution)/shard_map/all_to_all | solution.py:47
  153.5 3.5 %collective-permute-start.25 = (bf16[128,1024]{1,0:T(8,128)(2,1)S(1)}, bf16[128,1024]{1,0:T(8,128)(2,1)S(1)}, u32[]{:S(2)}, u32[]{:S(2)}) collective-permute-start(bf16[128,1024]{1,0:T(8,128)(2,1)S(1)} %fusion.1), channel_id=1, source_target_pairs={{0,128},{128,0},{1,129},{129,1},{2,130},{130,2},{3,131},{131,3},{4... | collective-permute-start | bytes 786440 | tf_op jit(solution)/shard_map/ppermute | solution.py:27
  157.3 6.4 %shard_map.94 = bf16[256,1024]{1,0:T(8,128)(2,1)S(1)} custom-call(bf16[64,4096]{1,0:T(8,128)(2,1)} %get-tuple-element.55.refs_0_, bf16[64,4096]{1,0:T(8,128)(2,1)} %collective-permute-done.14.refs_1_, bf16[64,4096]{1,0:T(8,128)(2,1)} %collective-permute-done.15.refs_2_, bf16[64,4096]{1,0:T(8,128)(2,1)} %collective-permute-done.18.refs_3_, ...), custom_call_target="tpu_custom_call" | custom-call | tf_op jit(solution)/shard_map/pallas_call | solution.py:66
  163.6 1.2 collective-permute-done.25
  165.0 2.3 all-to-all-done.4
  167.3 1.9 convolution_convert_fusion.refs_2_
  169.3 3.5 %collective-permute-start.27 = (bf16[256,1024]{1,0:T(8,128)(2,1)S(1)}, bf16[256,1024]{1,0:T(8,128)(2,1)S(1)}, u32[]{:S(2)}, u32[]{:S(2)}) collective-permute-start(bf16[256,1024]{1,0:T(8,128)(2,1)S(1)} %shard_map.94), channel_id=1, source_target_pairs={{0,128},{128,0},{1,129},{129,1},{2,130},{130,2},{3,131},{131,3},{4... | collective-permute-start | bytes 1572872 | tf_op jit(solution)/shard_map/ppermute | solution.py:27
  173.9 1.9 collective-permute-start.29
  175.9 1.6 collective-permute-start.28
  177.5 3.1 %shard_map.95 = bf16[16,1152]{1,0:T(8,128)(2,1)S(1)} custom-call(s32[7]{0:T(128)S(1)} %stack.27.refs_0_, f32[8,64,128]{2,1,0:T(8,128)S(1)} %all-to-all-done.2.refs_0_.refs_1_, bf16[512,1024]{1,0:T(8,128)(2,1)S(1)} %convolution_convert_fusion.refs_2_, bf16[512,1024]{1,0:T(8,128)(2,1)S(1)} %collective-permute-done.26.refs_3_, ...), custom_call_target="tpu_custom_call" | custom-call | tf_op jit(solution)/shard_map/pallas_call | solution.py:66
  180.5 7.3 %collective-permute-done.27.refs_5_ = bf16[256,1024]{1,0:T(8,128)(2,1)S(1)} collective-permute-done((bf16[256,1024]{1,0:T(8,128)(2,1)S(1)}, bf16[256,1024]{1,0:T(8,128)(2,1)S(1)}, u32[]{:S(2)}, u32[]{:S(2)}) %collective-permute-start.27) | collective-permute-done | bytes 524320 | tf_op jit(solution)/shard_map/ppermute | solution.py:27
  188.9 18.6 %all-to-all-start.5 = ((bf16[16,16,1152]{2,1,0:T(8,128)(2,1)}), bf16[16,16,1152]{2,1,0:T(8,128)(2,1)S(1)}, u32[]{:S(2)}, u32[]{:S(2)}) async-start(bf16[16,16,1152]{2,1,0:T(8,128)(2,1)} %broadcast_in_dim.20), calls=%async_computation.5 | async-start | bytes 1179648 | tf_op jit(solution)/shard_map/all_to_all | solution.py:47
  211.8 5.8 %shard_map.97.refs_4_ = f32[256,1024]{1,0:T(8,128)S(1)} custom-call(bf16[64,4096]{1,0:T(8,128)(2,1)S(1)} %get-tuple-element.56.refs_0_, bf16[64,4096]{1,0:T(8,128)(2,1)S(1)} %copy-done.7, bf16[64,4096]{1,0:T(8,128)(2,1)S(1)} %copy-done.9, bf16[64,4096]{1,0:T(8,128)(2,1)S(1)} %copy-done.11, bf16[4096,512]{1,0:T(8,128)(2,1)} %shard_map.92.refs_6_.refs_4_, ...), custom_call_target="tpu_custom_call" | custom-call | tf_op jit(solution)/shard_map/pallas_call | solution.py:66
  218.6 5.7 %all-to-all-done.5.refs_1_ = bf16[16,16,1152]{2,1,0:T(8,128)(2,1)S(1)} async-done(((bf16[16,16,1152]{2,1,0:T(8,128)(2,1)}), bf16[16,16,1152]{2,1,0:T(8,128)(2,1)S(1)}, u32[]{:S(2)}, u32[]{:S(2)}) %all-to-all-start.5) | async-done | bytes 589856 | tf_op jit(solution)/shard_map/all_to_all | solution.py:47
  224.3 1.2 copy-done.5
  226.6 1.7 shard_map.98
  228.3 13.4 %all_to_all.39.refs_0_ = f32[16,16,128]{2,1,0:T(8,128)S(1)} all-to-all(f32[16,16,128]{2,1,0:T(8,128)S(1)} %shard_map.98), channel_id=1, replica_groups=mesh['zhi'=2,'x'=4,'zlo'=4,'y'=4,'core'=2] {'zlo','y'}, dimensions={0} | all-to-all | bytes 262144 | tf_op jit(solution)/shard_map/all_to_all | solution.py:513
  (120 shorter events, 27.4 us)
Async XLA Ops:
  0.0 32.0 %copy-start.25 = (s32[32]{0:T(128)S(1)}, s32[32]{0:T(128)}, u32[]{:S(2)}) copy-start(s32[32]{0:T(128)} %refs_1_.1) | copy-start | bytes 388
  0.0 32.0 %copy-start.24 = (s32[32,128]{1,0:T(8,128)S(1)}, s32[32,128]{1,0:T(8,128)}, u32[]{:S(2)}) copy-start(s32[32,128]{1,0:T(8,128)} %refs_3_.1) | copy-start | bytes 49156
  2.0 21.5 %collective-permute-start.2 = (bf16[256,256]{1,0:T(8,128)(2,1)S(1)}, bf16[256,256]{1,0:T(8,128)(2,1)S(1)}, u32[]{:S(2)}, u32[]{:S(2)}) collective-permute-start(bf16[256,256]{1,0:T(8,128)(2,1)S(1)} %pad_maximum_fusion), channel_id=1, source_target_pairs={{0,24},{8,16},{16,8},{24,0},{1,25},{9,17},{17,9},{25,1},{2,26},{10... | collective-permute-start | bytes 393224 | tf_op jit(solution)/shard_map/ppermute | solution.py:27
  6.7 16.8 %collective-permute-start.1 = (bf16[256,256]{1,0:T(8,128)(2,1)S(1)}, bf16[256,256]{1,0:T(8,128)(2,1)S(1)}, u32[]{:S(2)}, u32[]{:S(2)}) collective-permute-start(bf16[256,256]{1,0:T(8,128)(2,1)S(1)} %pad_maximum_fusion), channel_id=1, source_target_pairs={{0,16},{8,24},{16,0},{24,8},{1,17},{9,25},{17,1},{25,9},{2,18},{10... | collective-permute-start | bytes 393224 | tf_op jit(solution)/shard_map/ppermute | solution.py:27
  6.7 16.8 %collective-permute-start = (bf16[256,256]{1,0:T(8,128)(2,1)S(1)}, bf16[256,256]{1,0:T(8,128)(2,1)S(1)}, u32[]{:S(2)}, u32[]{:S(2)}) collective-permute-start(bf16[256,256]{1,0:T(8,128)(2,1)S(1)} %pad_maximum_fusion), channel_id=1, source_target_pairs={{0,8},{8,0},{16,24},{24,16},{1,9},{9,1},{17,25},{25,17},{2,10},{10... | collective-permute-start | bytes 393224 | tf_op jit(solution)/shard_map/ppermute | solution.py:27
  7.4 16.1 %all-to-all-start = ((bf16[16,8,256]{2,1,0:T(8,128)(2,1)}), bf16[16,8,256]{2,1,0:T(8,128)(2,1)S(1)}, u32[]{:S(2)}, u32[]{:S(2)}) async-start(bf16[16,8,256]{2,1,0:T(8,128)(2,1)} %bitcast.26), calls=%async_computation | async-start | bytes 131072 | tf_op jit(solution)/shard_map/all_to_all | solution.py:391
  24.2 14.0 %collective-permute-start.3 = (bf16[2,256,128]{2,1,0:T(8,128)(2,1)S(1)}, bf16[2,256,128]{2,1,0:T(8,128)(2,1)}, u32[]{:S(2)}, u32[]{:S(2)}) collective-permute-start(bf16[2,256,128]{2,1,0:T(8,128)(2,1)S(1)} %shard_map.84), channel_id=1, source_target_pairs={{0,128},{128,0},{1,129},{129,1},{2,130},{130,2},{3,131},{131,3},{4... | collective-permute-start | bytes 393224 | tf_op jit(solution)/shard_map/ppermute | solution.py:27
  28.7 29.7 %collective-permute-start.7 = (bf16[4,256,256]{2,1,0:T(8,128)(2,1)S(1)}, bf16[4,256,256]{2,1,0:T(8,128)(2,1)S(1)}, u32[]{:S(2)}, u32[]{:S(2)}) collective-permute-start(bf16[4,256,256]{2,1,0:T(8,128)(2,1)S(1)} %shard_map.83.refs_1_.refs_4_), channel_id=1, source_target_pairs={{0,4},{2,6},{4,0},{6,2},{1,5},{3,7},{5,1},{7,3},{8,12},{10,14},{12... | collective-permute-start | bytes 1572872 | tf_op jit(solution)/shard_map/ppermute | solution.py:27
  29.7 28.7 %collective-permute-start.6 = (bf16[4,256,256]{2,1,0:T(8,128)(2,1)S(1)}, bf16[4,256,256]{2,1,0:T(8,128)(2,1)}, u32[]{:S(2)}, u32[]{:S(2)}) collective-permute-start(bf16[4,256,256]{2,1,0:T(8,128)(2,1)S(1)} %shard_map.83.refs_1_.refs_4_), channel_id=1, source_target_pairs={{0,6},{2,4},{4,2},{6,0},{1,7},{3,5},{5,3},{7,1},{8,14},{10,12},{12... | collective-permute-start | bytes 1572872 | tf_op jit(solution)/shard_map/ppermute | solution.py:27
  32.0 1.6 copy-start.1
  38.2 23.9 %collective-permute-start.4 = (bf16[128,4096]{1,0:T(8,128)(2,1)}, bf16[128,4096]{1,0:T(8,128)(2,1)}, u32[]{:S(2)}, u32[]{:S(2)}) collective-permute-start(bf16[128,4096]{1,0:T(8,128)(2,1)} %get-tuple-element.44), channel_id=1, source_target_pairs={{0,1},{1,0},{2,3},{3,2},{4,5},{5,4},{6,7},{7,6},{8,9},{9,8},{10,11... | collective-permute-start | bytes 3145736 | tf_op jit(solution)/shard_map/ppermute | solution.py:27
  40.8 21.1 %collective-permute-start.5 = (bf16[4,256,256]{2,1,0:T(8,128)(2,1)S(1)}, bf16[4,256,256]{2,1,0:T(8,128)(2,1)}, u32[]{:S(2)}, u32[]{:S(2)}) collective-permute-start(bf16[4,256,256]{2,1,0:T(8,128)(2,1)S(1)} %shard_map.83.refs_1_.refs_4_), channel_id=1, source_target_pairs={{0,2},{2,0},{4,6},{6,4},{1,3},{3,1},{5,7},{7,5},{8,10},{10,8},{12,... | collective-permute-start | bytes 1572872 | tf_op jit(solution)/shard_map/ppermute | solution.py:27
  41.1 14.4 %collective-permute-start.12 = (bf16[32,4096]{1,0:T(8,128)(2,1)S(1)}, bf16[32,4096]{1,0:T(8,128)(2,1)S(1)}, u32[]{:S(2)}, u32[]{:S(2)}) collective-permute-start(bf16[32,4096]{1,0:T(8,128)(2,1)S(1)} %shard_map.88.refs_0_), channel_id=1, source_target_pairs={{0,8},{8,0},{16,24},{24,16},{1,9},{9,1},{17,25},{25,17},{2,10},{10... | collective-permute-start | bytes 786440 | tf_op jit(solution)/shard_map/ppermute | solution.py:27
  41.3 20.9 %all-to-all-start.1 = ((bf16[8,8,4096]{2,1,0:T(8,128)(2,1)}), bf16[8,8,4096]{2,1,0:T(8,128)(2,1)S(1)}, u32[]{:S(2)}, u32[]{:S(2)}) async-start(bf16[8,8,4096]{2,1,0:T(8,128)(2,1)} %shard_map.85), calls=%async_computation.1 | async-start | bytes 1048576 | tf_op jit(solution)/shard_map/all_to_all | solution.py:436
  56.2 36.9 %collective-permute-start.22 = (bf16[1024,512]{1,0:T(8,128)(2,1)S(1)}, bf16[1024,512]{1,0:T(8,128)(2,1)}, u32[]{:S(2)}, u32[]{:S(2)}) collective-permute-start(bf16[1024,512]{1,0:T(8,128)(2,1)S(1)} %multiply_convert_fusion.refs_0_), channel_id=1, source_target_pairs={{0,64},{32,96},{64,0},{96,32},{1,65},{33,97},{65,1},{97,33},{2,66}... | collective-permute-start | bytes 3145736 | tf_op jit(solution)/shard_map/ppermute | solution.py:27
  58.4 43.3 %collective-permute-start.21 = (bf16[1024,512]{1,0:T(8,128)(2,1)S(1)}, bf16[1024,512]{1,0:T(8,128)(2,1)}, u32[]{:S(2)}, u32[]{:S(2)}) collective-permute-start(bf16[1024,512]{1,0:T(8,128)(2,1)S(1)} %multiply_convert_fusion.refs_0_), channel_id=1, source_target_pairs={{0,96},{32,64},{64,32},{96,0},{1,97},{33,65},{65,33},{97,1},{2,98}... | collective-permute-start | bytes 3145736 | tf_op jit(solution)/shard_map/ppermute | solution.py:27
  58.4 43.4 %collective-permute-start.20 = (bf16[1024,512]{1,0:T(8,128)(2,1)S(1)}, bf16[1024,512]{1,0:T(8,128)(2,1)}, u32[]{:S(2)}, u32[]{:S(2)}) collective-permute-start(bf16[1024,512]{1,0:T(8,128)(2,1)S(1)} %multiply_convert_fusion.refs_0_), channel_id=1, source_target_pairs={{0,32},{32,0},{64,96},{96,64},{1,33},{33,1},{65,97},{97,65},{2,34}... | collective-permute-start | bytes 3145736 | tf_op jit(solution)/shard_map/ppermute | solution.py:27
  62.0 24.4 %collective-permute-start.13 = (bf16[64,4096]{1,0:T(8,128)(2,1)S(1)}, bf16[64,4096]{1,0:T(8,128)(2,1)}, u32[]{:S(2)}, u32[]{:S(2)}) collective-permute-start(bf16[64,4096]{1,0:T(8,128)(2,1)S(1)} %shard_map.89.refs_0_), channel_id=1, source_target_pairs={{0,16},{8,24},{16,0},{24,8},{1,17},{9,25},{17,1},{25,9},{2,18},{10... | collective-permute-start | bytes 1572872 | tf_op jit(solution)/shard_map/ppermute | solution.py:27
  62.1 6.8 %collective-permute-start.11 = (bf16[2,256,128]{2,1,0:T(8,128)(2,1)}, bf16[2,256,128]{2,1,0:T(8,128)(2,1)S(1)}, u32[]{:S(2)}, u32[]{:S(2)}) collective-permute-start(bf16[2,256,128]{2,1,0:T(8,128)(2,1)} %collective-permute-done.3.refs_2_), channel_id=1, source_target_pairs={{0,4},{2,6},{4,0},{6,2},{1,5},{3,7},{5,1},{7,3},{8,12},{10,14},{12... | collective-permute-start | bytes 393224 | tf_op jit(solution)/shard_map/ppermute | solution.py:27
  65.8 35.9 %copy-start.12 = (bf16[8,256,128]{2,1,0:T(8,128)(2,1)}, bf16[8,256,128]{2,1,0:T(8,128)(2,1)S(1)}, u32[]{:S(2)}) copy-start(bf16[8,256,128]{2,1,0:T(8,128)(2,1)S(1)} %get-tuple-element.60.refs_1_) | copy-start | bytes 1572868
  69.5 17.8 %collective-permute-start.8 = (f32[288,128]{1,0:T(8,128)S(1)}, f32[288,128]{1,0:T(8,128)S(1)}, u32[]{:S(2)}, u32[]{:S(2)}) collective-permute-start(f32[288,128]{1,0:T(8,128)S(1)} %get-tuple-element.49), channel_id=1, source_target_pairs={{0,1},{1,0},{2,3},{3,2},{4,5},{5,4},{6,7},{7,6},{8,9},{9,8},{10,11... | collective-permute-start | bytes 442376 | tf_op jit(solution)/shard_map/ppermute | solution.py:27
  86.4 6.8 %collective-permute-start.10 = (bf16[2,256,128]{2,1,0:T(8,128)(2,1)}, bf16[2,256,128]{2,1,0:T(8,128)(2,1)S(1)}, u32[]{:S(2)}, u32[]{:S(2)}) collective-permute-start(bf16[2,256,128]{2,1,0:T(8,128)(2,1)} %collective-permute-done.3.refs_2_), channel_id=1, source_target_pairs={{0,6},{2,4},{4,2},{6,0},{1,7},{3,5},{5,3},{7,1},{8,14},{10,12},{12... | collective-permute-start | bytes 393224 | tf_op jit(solution)/shard_map/ppermute | solution.py:27
  87.2 5.9 %collective-permute-start.9 = (bf16[2,256,128]{2,1,0:T(8,128)(2,1)}, bf16[2,256,128]{2,1,0:T(8,128)(2,1)S(1)}, u32[]{:S(2)}, u32[]{:S(2)}) collective-permute-start(bf16[2,256,128]{2,1,0:T(8,128)(2,1)} %collective-permute-done.3.refs_2_), channel_id=1, source_target_pairs={{0,2},{2,0},{4,6},{6,4},{1,3},{3,1},{5,7},{7,5},{8,10},{10,8},{12,... | collective-permute-start | bytes 393224 | tf_op jit(solution)/shard_map/ppermute | solution.py:27
  93.2 45.1 %copy-start.21 = (bf16[2,256,128]{2,1,0:T(8,128)(2,1)S(1)}, bf16[2,256,128]{2,1,0:T(8,128)(2,1)}, u32[]{:S(2)}) copy-start(bf16[2,256,128]{2,1,0:T(8,128)(2,1)} %copy-done.20) | copy-start | bytes 393220
  101.9 36.4 %copy-start.13 = (bf16[8,256,128]{2,1,0:T(8,128)(2,1)S(1)}, bf16[8,256,128]{2,1,0:T(8,128)(2,1)}, u32[]{:S(2)}) copy-start(bf16[8,256,128]{2,1,0:T(8,128)(2,1)} %copy-done.12) | copy-start | bytes 1572868
  106.0 32.2 %collective-permute-start.23 = (bf16[4096,512]{1,0:T(8,128)(2,1)}, bf16[4096,512]{1,0:T(8,128)(2,1)}, u32[]{:S(2)}, u32[]{:S(2)}) collective-permute-start(bf16[4096,512]{1,0:T(8,128)(2,1)} %shard_map.92.refs_6_.refs_4_), channel_id=1, source_target_pairs={{0,1},{1,0},{2,3},{3,2},{4,5},{5,4},{6,7},{7,6},{8,9},{9,8},{10,11... | collective-permute-start | bytes 12582920 | tf_op jit(solution)/shard_map/ppermute | solution.py:27
  106.0 16.2 %collective-permute-start.15 = (bf16[64,4096]{1,0:T(8,128)(2,1)}, bf16[64,4096]{1,0:T(8,128)(2,1)}, u32[]{:S(2)}, u32[]{:S(2)}) collective-permute-start(bf16[64,4096]{1,0:T(8,128)(2,1)} %get-tuple-element.55.refs_0_), channel_id=1, source_target_pairs={{0,6},{2,4},{4,2},{6,0},{1,7},{3,5},{5,3},{7,1},{8,14},{10,12},{12... | collective-permute-start | bytes 1572872 | tf_op jit(solution)/shard_map/ppermute | solution.py:27
  107.2 15.6 %collective-permute-start.16 = (bf16[64,4096]{1,0:T(8,128)(2,1)S(1)}, bf16[64,4096]{1,0:T(8,128)(2,1)S(1)}, u32[]{:S(2)}, u32[]{:S(2)}) collective-permute-start(bf16[64,4096]{1,0:T(8,128)(2,1)S(1)} %get-tuple-element.56.refs_0_), channel_id=1, source_target_pairs={{0,2},{2,0},{4,6},{6,4},{1,3},{3,1},{5,7},{7,5},{8,10},{10,8},{12,... | collective-permute-start | bytes 1572872 | tf_op jit(solution)/shard_map/ppermute | solution.py:27
  108.1 25.2 %collective-permute-start.14 = (bf16[64,4096]{1,0:T(8,128)(2,1)}, bf16[64,4096]{1,0:T(8,128)(2,1)}, u32[]{:S(2)}, u32[]{:S(2)}) collective-permute-start(bf16[64,4096]{1,0:T(8,128)(2,1)} %get-tuple-element.55.refs_0_), channel_id=1, source_target_pairs={{0,2},{2,0},{4,6},{6,4},{1,3},{3,1},{5,7},{7,5},{8,10},{10,8},{12,... | collective-permute-start | bytes 1572872 | tf_op jit(solution)/shard_map/ppermute | solution.py:27
  109.3 24.1 %collective-permute-start.17 = (bf16[64,4096]{1,0:T(8,128)(2,1)S(1)}, bf16[64,4096]{1,0:T(8,128)(2,1)S(1)}, u32[]{:S(2)}, u32[]{:S(2)}) collective-permute-start(bf16[64,4096]{1,0:T(8,128)(2,1)S(1)} %get-tuple-element.56.refs_0_), channel_id=1, source_target_pairs={{0,6},{2,4},{4,2},{6,0},{1,7},{3,5},{5,3},{7,1},{8,14},{10,12},{12... | collective-permute-start | bytes 1572872 | tf_op jit(solution)/shard_map/ppermute | solution.py:27
  111.3 17.0 %all-to-all-start.2 = ((f32[8,64,128]{2,1,0:T(8,128)}), f32[8,64,128]{2,1,0:T(8,128)S(1)}, u32[]{:S(2)}, u32[]{:S(2)}) async-start(f32[8,64,128]{2,1,0:T(8,128)} %shard_map.87), calls=%async_computation.2 | async-start | bytes 524288 | tf_op jit(solution)/shard_map/all_to_all | solution.py:456
  122.3 24.7 %collective-permute-start.18 = (bf16[64,4096]{1,0:T(8,128)(2,1)}, bf16[64,4096]{1,0:T(8,128)(2,1)}, u32[]{:S(2)}, u32[]{:S(2)}) collective-permute-start(bf16[64,4096]{1,0:T(8,128)(2,1)} %collective-permute-done.15.refs_2_), channel_id=1, source_target_pairs={{0,2},{2,0},{4,6},{6,4},{1,3},{3,1},{5,7},{7,5},{8,10},{10,8},{12,... | collective-permute-start | bytes 1572872 | tf_op jit(solution)/shard_map/ppermute | solution.py:27
  122.8 20.9 %copy-start.6 = (bf16[64,4096]{1,0:T(8,128)(2,1)}, bf16[64,4096]{1,0:T(8,128)(2,1)S(1)}, u32[]{:S(2)}) copy-start(bf16[64,4096]{1,0:T(8,128)(2,1)S(1)} %collective-permute-done.16.refs_1_) | copy-start | bytes 1572868
  122.8 24.1 %collective-permute-start.19 = (bf16[64,4096]{1,0:T(8,128)(2,1)S(1)}, bf16[64,4096]{1,0:T(8,128)(2,1)S(1)}, u32[]{:S(2)}, u32[]{:S(2)}) collective-permute-start(bf16[64,4096]{1,0:T(8,128)(2,1)S(1)} %collective-permute-done.16.refs_1_), channel_id=1, source_target_pairs={{0,6},{2,4},{4,2},{6,0},{1,7},{3,5},{5,3},{7,1},{8,14},{10,12},{12... | collective-permute-start | bytes 1572872 | tf_op jit(solution)/shard_map/ppermute | solution.py:27
  133.4 4.8 %copy-start.8 = (bf16[64,4096]{1,0:T(8,128)(2,1)}, bf16[64,4096]{1,0:T(8,128)(2,1)S(1)}, u32[]{:S(2)}) copy-start(bf16[64,4096]{1,0:T(8,128)(2,1)S(1)} %collective-permute-done.17.refs_2_) | copy-start | bytes 1572868
  134.2 12.8 %all-to-all-start.3 = ((bf16[4,32,1024]{2,1,0:T(8,128)(2,1)}), bf16[4,32,1024]{2,1,0:T(8,128)(2,1)}, u32[]{:S(2)}, u32[]{:S(2)}) async-start(bf16[4,32,1024]{2,1,0:T(8,128)(2,1)} %broadcast_in_dim.18), calls=%async_computation.3 | async-start | bytes 524288 | tf_op jit(solution)/shard_map/all_to_all | solution.py:47
  143.8 9.7 %collective-permute-start.24 = (bf16[128,1024]{1,0:T(8,128)(2,1)}, bf16[128,1024]{1,0:T(8,128)(2,1)S(1)}, u32[]{:S(2)}, u32[]{:S(2)}) collective-permute-start(bf16[128,1024]{1,0:T(8,128)(2,1)} %get-tuple-element.67), channel_id=1, source_target_pairs={{0,1},{1,0},{2,3},{3,2},{4,5},{5,4},{6,7},{7,6},{8,9},{9,8},{10,11... | collective-permute-start | bytes 786440 | tf_op jit(solution)/shard_map/ppermute | solution.py:27
  146.9 6.5 %copy-start.10 = (bf16[64,4096]{1,0:T(8,128)(2,1)}, bf16[64,4096]{1,0:T(8,128)(2,1)S(1)}, u32[]{:S(2)}) copy-start(bf16[64,4096]{1,0:T(8,128)(2,1)S(1)} %collective-permute-done.19.refs_3_) | copy-start | bytes 1572868
  149.2 18.1 %all-to-all-start.4 = ((bf16[4,4,32,1024]{3,2,1,0:T(8,128)(2,1)}), bf16[4,4,32,1024]{3,2,1,0:T(8,128)(2,1)}, u32[]{:S(2)}, u32[]{:S(2)}) async-start(bf16[4,4,32,1024]{3,2,1,0:T(8,128)(2,1)} %broadcast_in_dim.19), calls=%async_computation.4 | async-start | bytes 2097152 | tf_op jit(solution)/shard_map/all_to_all | solution.py:47
  153.5 11.4 %collective-permute-start.25 = (bf16[128,1024]{1,0:T(8,128)(2,1)S(1)}, bf16[128,1024]{1,0:T(8,128)(2,1)S(1)}, u32[]{:S(2)}, u32[]{:S(2)}) collective-permute-start(bf16[128,1024]{1,0:T(8,128)(2,1)S(1)} %fusion.1), channel_id=1, source_target_pairs={{0,128},{128,0},{1,129},{129,1},{2,130},{130,2},{3,131},{131,3},{4... | collective-permute-start | bytes 786440 | tf_op jit(solution)/shard_map/ppermute | solution.py:27
  169.2 8.3 %collective-permute-start.26 = (bf16[512,1024]{1,0:T(8,128)(2,1)S(1)}, bf16[512,1024]{1,0:T(8,128)(2,1)S(1)}, u32[]{:S(2)}, u32[]{:S(2)}) collective-permute-start(bf16[512,1024]{1,0:T(8,128)(2,1)S(1)} %convolution_convert_fusion.refs_2_), channel_id=1, source_target_pairs={{0,1},{1,0},{2,3},{3,2},{4,5},{5,4},{6,7},{7,6},{8,9},{9,8},{10,11... | collective-permute-start | bytes 3145736 | tf_op jit(solution)/shard_map/ppermute | solution.py:27
  169.3 18.5 %collective-permute-start.27 = (bf16[256,1024]{1,0:T(8,128)(2,1)S(1)}, bf16[256,1024]{1,0:T(8,128)(2,1)S(1)}, u32[]{:S(2)}, u32[]{:S(2)}) collective-permute-start(bf16[256,1024]{1,0:T(8,128)(2,1)S(1)} %shard_map.94), channel_id=1, source_target_pairs={{0,128},{128,0},{1,129},{129,1},{2,130},{130,2},{3,131},{131,3},{4... | collective-permute-start | bytes 1572872 | tf_op jit(solution)/shard_map/ppermute | solution.py:27
  172.8 15.0 %collective-permute-start.30 = (bf16[128,1024]{1,0:T(8,128)(2,1)S(1)}, bf16[128,1024]{1,0:T(8,128)(2,1)S(1)}, u32[]{:S(2)}, u32[]{:S(2)}) collective-permute-start(bf16[128,1024]{1,0:T(8,128)(2,1)S(1)} %add_convert_fusion.refs_0_), channel_id=1, source_target_pairs={{0,64},{32,96},{64,0},{96,32},{1,65},{33,97},{65,1},{97,33},{2,66}... | collective-permute-start | bytes 786440 | tf_op jit(solution)/shard_map/ppermute | solution.py:27
  173.9 13.9 %collective-permute-start.29 = (bf16[128,1024]{1,0:T(8,128)(2,1)S(1)}, bf16[128,1024]{1,0:T(8,128)(2,1)S(1)}, u32[]{:S(2)}, u32[]{:S(2)}) collective-permute-start(bf16[128,1024]{1,0:T(8,128)(2,1)S(1)} %add_convert_fusion.refs_0_), channel_id=1, source_target_pairs={{0,96},{32,64},{64,32},{96,0},{1,97},{33,65},{65,33},{97,1},{2,98}... | collective-permute-start | bytes 786440 | tf_op jit(solution)/shard_map/ppermute | solution.py:27
  175.9 12.0 %collective-permute-start.28 = (bf16[128,1024]{1,0:T(8,128)(2,1)S(1)}, bf16[128,1024]{1,0:T(8,128)(2,1)S(1)}, u32[]{:S(2)}, u32[]{:S(2)}) collective-permute-start(bf16[128,1024]{1,0:T(8,128)(2,1)S(1)} %add_convert_fusion.refs_0_), channel_id=1, source_target_pairs={{0,32},{32,0},{64,96},{96,64},{1,33},{33,1},{65,97},{97,65},{2,34}... | collective-permute-start | bytes 786440 | tf_op jit(solution)/shard_map/ppermute | solution.py:27
  188.9 35.4 %all-to-all-start.5 = ((bf16[16,16,1152]{2,1,0:T(8,128)(2,1)}), bf16[16,16,1152]{2,1,0:T(8,128)(2,1)S(1)}, u32[]{:S(2)}, u32[]{:S(2)}) async-start(bf16[16,16,1152]{2,1,0:T(8,128)(2,1)} %broadcast_in_dim.20), calls=%async_computation.5 | async-start | bytes 1179648 | tf_op jit(solution)/shard_map/all_to_all | solution.py:47
  208.5 9.0 %collective-permute-start.31 = (bf16[512,1024]{1,0:T(8,128)(2,1)S(1)}, bf16[512,1024]{1,0:T(8,128)(2,1)S(1)}, u32[]{:S(2)}, u32[]{:S(2)}) collective-permute-start(bf16[512,1024]{1,0:T(8,128)(2,1)S(1)} %shard_map.96.refs_2_), channel_id=1, source_target_pairs={{0,1},{1,0},{2,3},{3,2},{4,5},{5,4},{6,7},{7,6},{8,9},{9,8},{10,11... | collective-permute-start | bytes 3145736 | tf_op jit(solution)/shard_map/ppermute | solution.py:27
  211.8 12.5 %copy-start.23 = (s32[256,1]{1,0:T(8,128)S(1)}, s32[256,1]{1,0:T(8,128)}, u32[]{:S(2)}) copy-start(s32[256,1]{1,0:T(8,128)} %copy-done.22) | copy-start | bytes 3076
  (16 other events, 15.8 us)
